TPU v7x, 512 devices: a whole 4x4x16 slice. The times are simulated.
512 devices in a mesh: section: 32 (over y, x, core), dp: 16 (over z).
Axes of the slice: x: 4, y: 4, z: 16, core: 2. Of those that a mesh axis runs over, the one named last changes fastest.
Arguments:
- saved: bfloat16 [32, 16, 4, 2, 32, 4096], P('section', 'dp'), may hold values from -6 to 6
- incoming: bfloat16 [32, 16, 2, 32, 4096], P('section', 'dp'), may hold values from -6 to 6
- head: bfloat16 [3, 16, 32, 4096], P(None, 'dp'), may hold values from -6 to 6
- down_weight: bfloat16 [32, 4096, 256], P('section', 'dp'), may hold values from -0.09375 to 0.09375
- up_weight: bfloat16 [32, 4096, 256], P('section', 'dp'), may hold values from -0.1875 to 0.1875
- adopt: int32 [32, 16, 4], replicated, may hold values from -1 to 1, as said below
- live: int32 [16], replicated, may hold values from 0 to 1, as said below
Outputs:
- leaving: bfloat16 [32, 16, 2, 32, 4096], P('section', 'dp')
- grad_up: bfloat16 [32, 4096, 256], P('section', 'dp')
Inputs may be any that keep to these rules, and one draw needn't show every extreme that they name: `adopt`: values -1, 0, 1. A device (s, p) has either all 4 entries 0 or all nonzero (it failed); failed devices of one section are 4 or more relays apart on the cycle, so a device adopts at most one micro-batch in a step; every section has a failed device, and some device adopts in every step. `live`: both values occur.
All inputs are finite; a program needn't handle non-finite values.
Results may differ from a plain program's by a relative error of at most 0.019.
Values may be sent and summed in bfloat16 or wider, within the bound.
A program may use at most 64 MiB of HBM per device.

v0:
```python
import math

import jax
import jax.numpy as jnp
from jax import lax
from jax.sharding import PartitionSpec as P


def extended(block, sides, width):
    for axis, dim in sides:
        count = lax.axis_size(axis)
        forward = [(i, i + 1) for i in range(count - 1)]
        forward.append((count - 1, 0))
        backward = [(target, source) for source, target in forward]
        low = lax.ppermute(
            lax.slice_in_dim(block, block.shape[dim] - width, None, axis=dim), axis, forward
        )
        high = lax.ppermute(lax.slice_in_dim(block, 0, width, axis=dim), axis, backward)
        block = jnp.concatenate([low, block, high], axis=dim)
    return block


def passed_along(block, axis, distance):
    devices = range(lax.axis_size(axis))
    route = [(i - distance, i) for i in devices if i - distance in devices]
    return lax.ppermute(block, axis, route)


def contract_rows(left, right):
    return lax.dot_general(
        left, right, (((0,), (0,)), ((), ())), preferred_element_type=jnp.float32
    )


def body(saved, incoming, head, down_weight, up_weight, adopt, live):
    section_id = lax.axis_index("section")
    pipe_id = lax.axis_index("dp")
    n_section = lax.axis_size("section")
    n_pipe = lax.axis_size("dp")
    step_count = saved.shape[2]
    row_count = saved.shape[4]
    features = saved.shape[5]
    bottleneck = down_weight.shape[2]
    full_down, full_up = (
        lax.all_gather(down_weight, "dp", axis=1, tiled=True),
        lax.all_gather(up_weight, "dp", axis=1, tiled=True),
    )
    w_down = full_down[0]
    w_up = full_up[0]
    plan_row = adopt[section_id]
    here_plan = plan_row[pipe_id]
    left_plan = plan_row[(pipe_id - 1) % n_pipe]
    right_plan = plan_row[(pipe_id + 1) % n_pipe]
    activations = saved[0, 0]
    slot_grads = incoming[0, 0]
    acc_up = jnp.zeros((features, bottleneck), jnp.float32)
    outflow = slot_grads.reshape(2 * row_count, features)
    for step_index in range(step_count):
        keep_own = here_plan[step_index] == 0
        keep_adopted = (left_plan[step_index] == 1) | (right_plan[step_index] == -1)
        slot_mask = jnp.stack([keep_own, keep_adopted]).astype(jnp.bfloat16)[:, None, None]
        grads_flat = (slot_grads * slot_mask).reshape(2 * row_count, features)
        inputs = activations[step_index].reshape(2 * row_count, features)
        hidden = jnp.dot(inputs, w_down, preferred_element_type=jnp.float32)
        gate_sigmoid = jax.nn.sigmoid(hidden)
        active = (hidden * gate_sigmoid).astype(jnp.bfloat16)
        coupled = jnp.dot(grads_flat, w_up, preferred_element_type=jnp.float32)
        inner_grad = (gate_sigmoid * (1.0 + hidden * (1.0 - gate_sigmoid)) * coupled).astype(
            jnp.bfloat16
        )
        returned = lax.dot_general(
            inner_grad, w_down, (((1,), (1,)), ((), ())), preferred_element_type=jnp.float32
        )
        outflow = (grads_flat.astype(jnp.float32) + returned).astype(jnp.bfloat16)
        acc_up = acc_up + contract_rows(grads_flat, active)
        if step_index + 1 < step_count:
            pieces = outflow.reshape(2, row_count, features)
            beside_all = extended(pieces[1:2], (("dp", 0),), 1)
            direction = here_plan[step_index]
            home_grad = jnp.where(
                direction == 0, pieces[0], jnp.where(direction == 1, beside_all[2], beside_all[0])
            )
            from_above = passed_along(home_grad, "section", -1)
            from_above = jnp.where(section_id == n_section - 1, head[step_index, 0], from_above)
            neighbours = extended(from_above[None], (("dp", 0),), 1)
            adopted = jnp.where(left_plan[step_index + 1] == 1, neighbours[0], neighbours[2])
            slot_grads = jnp.stack([from_above, adopted])
    leaving = outflow.reshape(1, 1, 2, row_count, features)
    live_here = live[pipe_id].astype(jnp.float32)
    norm_factor = 1.0 / math.sqrt(n_pipe * step_count * row_count)
    partial_value = acc_up * live_here
    summed = lax.psum_scatter(
        partial_value.astype(jnp.bfloat16), "dp", scatter_dimension=0, tiled=True
    ).astype(jnp.float32)
    grad_up = (summed * norm_factor).astype(jnp.bfloat16)[None]
    return (leaving, grad_up)


def solution(mesh):
    placed = (
        P("section", "dp", None, None, None, None),
        P("section", "dp", None, None, None),
        P(None, "dp", None, None),
        P("section", "dp", None),
        P("section", "dp", None),
        P(),
        P(),
    )
    return jax.shard_map(
        body,
        mesh=mesh,
        in_specs=placed,
        out_specs=(P("section", "dp", None, None, None), P("section", "dp", None)),
        check_vma=False,
    )
```

profile of v0, /device:TPU:4, one launch (start us, length us, event | category | flops | bytes accessed | tf_op | source)
XLA Modules:
  0.0 369.8 jit_solution(5231984228338887944)
XLA Ops:
  13.0 1.9 broadcast_multiply_fusion.3
  17.2 70.4 %all-gather.3.cloned.1.call-done = bf16[1,4096,256]{2,1,0:T(8,128)(2,1)} async-done(((bf16[1,256,256]{2,1,0:T(8,128)(2,1)}), bf16[1,4096,256]{2,1,0:T(8,128)(2,1)}) %all-gather.3.cloned.1.call-update) | async-done | bytes 2097168 | tf_op jit(solution)/shard_map/all_gather | solution.py:45
  87.7 2.2 fusion.24
  89.9 70.0 %all-gather.5.cloned.1.call-done = bf16[1,4096,256]{2,1,0:T(8,128)(2,1)} async-done(((bf16[1,256,256]{2,1,0:T(8,128)(2,1)}), bf16[1,4096,256]{2,1,0:T(8,128)(2,1)}) %all-gather.5.cloned.1.call-update) | async-done | bytes 2097168 | tf_op jit(solution)/shard_map/all_gather | solution.py:46
  159.8 3.4 fusion.2
  163.3 3.7 collective-permute-start.1
  167.0 3.4 collective-permute-start
  172.7 2.5 collective-permute-done
  175.3 1.9 collective-permute-start.2
  182.1 4.6 %collective-permute-start.4 = (bf16[1,32,4096]{2,1,0:T(8,128)(2,1)S(1)}, bf16[1,32,4096]{2,1,0:T(8,128)(2,1)S(1)}, u32[]{:S(2)}, u32[]{:S(2)}) collective-permute-start(bf16[1,32,4096]{2,1,0:T(8,128)(2,1)S(1)} %fusion.58), channel_id=1, source_target_pairs={{1,0},{2,1},{3,2},{4,3},{5,4},{6,5},{7,6},{8,7},{9,8},{10,9},{11,1... | collective-permute-start | bytes 786440 | tf_op jit(solution)/shard_map/ppermute | solution.py:18
  186.6 1.9 collective-permute-start.3
  190.1 2.8 collective-permute-done.4
  192.9 5.8 %collective-permute-done.3 = bf16[1,32,4096]{2,1,0:T(8,128)(2,1)S(1)} collective-permute-done((bf16[1,32,4096]{2,1,0:T(8,128)(2,1)S(1)}, bf16[1,32,4096]{2,1,0:T(8,128)(2,1)S(1)}, u32[]{:S(2)}, u32[]{:S(2)}) %collective-permute-start.3) | collective-permute-done | bytes 262176 | tf_op jit(solution)/shard_map/ppermute | solution.py:15
  199.8 4.2 %fusion.3 = bf16[64,4096]{1,0:T(8,128)(2,1)} fusion(bf16[1,4096,256]{2,1,0:T(8,128)(2,1)S(1)} %copy-done, bf16[64,4096]{1,0:T(8,128)(2,1)} %bitcast.133, bf16[1,4096,256]{2,1,0:T(8,128)(2,1)} %all-gather.5.cloned.1.call-done, bf16[64,4096]{1,0:T(8,128)(2,1)S(1)} %bitcast_multiply_fusion.2, f32[64,256]{1,0:T(8,128)S(1)} %fusion.21), kind=kOutput, calls=%fused_computation.10 | convolution fusion | flops 269369344 | bytes 5832704 | tf_op jit(solution)/shard_map/dot_general | solution.py:71
  207.6 5.1 %collective-permute-start.5 = (bf16[1,32,4096]{2,1,0:T(8,128)(2,1)}, bf16[1,32,4096]{2,1,0:T(8,128)(2,1)}, u32[]{:S(2)}, u32[]{:S(2)}) collective-permute-start(bf16[1,32,4096]{2,1,0:T(8,128)(2,1)} %slice_bitcast_fusion.1), channel_id=1, source_target_pairs={{1,0},{2,1},{3,2},{4,3},{5,4},{6,5},{7,6},{8,7},{9,8},{10,9},{11,1... | collective-permute-start | bytes 786440 | tf_op jit(solution)/shard_map/ppermute | solution.py:18
  221.3 2.1 collective-permute-start.7
  223.4 2.7 fusion.78
  228.2 3.9 %collective-permute-start.9 = (bf16[1,32,4096]{2,1,0:T(8,128)(2,1)S(1)}, bf16[1,32,4096]{2,1,0:T(8,128)(2,1)S(1)}, u32[]{:S(2)}, u32[]{:S(2)}) collective-permute-start(bf16[1,32,4096]{2,1,0:T(8,128)(2,1)S(1)} %fusion.59), channel_id=1, source_target_pairs={{1,0},{2,1},{3,2},{4,3},{5,4},{6,5},{7,6},{8,7},{9,8},{10,9},{11,1... | collective-permute-start | bytes 786440 | tf_op jit(solution)/shard_map/ppermute | solution.py:18
  232.1 2.0 collective-permute-start.8
  234.6 4.3 %collective-permute-done.9 = bf16[1,32,4096]{2,1,0:T(8,128)(2,1)S(1)} collective-permute-done((bf16[1,32,4096]{2,1,0:T(8,128)(2,1)S(1)}, bf16[1,32,4096]{2,1,0:T(8,128)(2,1)S(1)}, u32[]{:S(2)}, u32[]{:S(2)}) %collective-permute-start.9) | collective-permute-done | bytes 262176 | tf_op jit(solution)/shard_map/ppermute | solution.py:18
  238.9 5.4 %collective-permute-done.8 = bf16[1,32,4096]{2,1,0:T(8,128)(2,1)S(1)} collective-permute-done((bf16[1,32,4096]{2,1,0:T(8,128)(2,1)S(1)}, bf16[1,32,4096]{2,1,0:T(8,128)(2,1)S(1)}, u32[]{:S(2)}, u32[]{:S(2)}) %collective-permute-start.8) | collective-permute-done | bytes 262176 | tf_op jit(solution)/shard_map/ppermute | solution.py:15
  245.4 4.2 %fusion.4 = bf16[64,4096]{1,0:T(8,128)(2,1)} fusion(bf16[1,4096,256]{2,1,0:T(8,128)(2,1)S(1)} %copy-done, bf16[64,4096]{1,0:T(8,128)(2,1)} %bitcast.134, bf16[1,4096,256]{2,1,0:T(8,128)(2,1)} %all-gather.5.cloned.1.call-done, bf16[64,4096]{1,0:T(8,128)(2,1)S(1)} %bitcast_multiply_fusion.1, f32[64,256]{1,0:T(8,128)S(1)} %fusion.18), kind=kOutput, calls=%fused_computation.11 | convolution fusion | flops 269369344 | bytes 5832704 | tf_op jit(solution)/shard_map/dot_general | solution.py:71
  250.7 2.1 collective-permute-start.11
  252.7 5.1 %collective-permute-start.10 = (bf16[1,32,4096]{2,1,0:T(8,128)(2,1)S(1)}, bf16[1,32,4096]{2,1,0:T(8,128)(2,1)S(1)}, u32[]{:S(2)}, u32[]{:S(2)}) collective-permute-start(bf16[1,32,4096]{2,1,0:T(8,128)(2,1)S(1)} %slice_bitcast_fusion), channel_id=1, source_target_pairs={{1,0},{2,1},{3,2},{4,3},{5,4},{6,5},{7,6},{8,7},{9,8},{10,9},{11,1... | collective-permute-start | bytes 786440 | tf_op jit(solution)/shard_map/ppermute | solution.py:18
  259.4 2.9 collective-permute-done.11
  267.1 3.1 collective-permute-done.12
  271.2 5.6 %collective-permute-start.14 = (bf16[1,32,4096]{2,1,0:T(8,128)(2,1)S(1)}, bf16[1,32,4096]{2,1,0:T(8,128)(2,1)S(1)}, u32[]{:S(2)}, u32[]{:S(2)}) collective-permute-start(bf16[1,32,4096]{2,1,0:T(8,128)(2,1)S(1)} %fusion.60), channel_id=1, source_target_pairs={{1,0},{2,1},{3,2},{4,3},{5,4},{6,5},{7,6},{8,7},{9,8},{10,9},{11,1... | collective-permute-start | bytes 786440 | tf_op jit(solution)/shard_map/ppermute | solution.py:18
  279.5 3.9 %collective-permute-done.14 = bf16[1,32,4096]{2,1,0:T(8,128)(2,1)S(1)} collective-permute-done((bf16[1,32,4096]{2,1,0:T(8,128)(2,1)S(1)}, bf16[1,32,4096]{2,1,0:T(8,128)(2,1)S(1)}, u32[]{:S(2)}, u32[]{:S(2)}) %collective-permute-start.14) | collective-permute-done | bytes 262176 | tf_op jit(solution)/shard_map/ppermute | solution.py:18
  283.3 5.3 %collective-permute-done.13 = bf16[1,32,4096]{2,1,0:T(8,128)(2,1)S(1)} collective-permute-done((bf16[1,32,4096]{2,1,0:T(8,128)(2,1)S(1)}, bf16[1,32,4096]{2,1,0:T(8,128)(2,1)S(1)}, u32[]{:S(2)}, u32[]{:S(2)}) %collective-permute-start.13) | collective-permute-done | bytes 262176 | tf_op jit(solution)/shard_map/ppermute | solution.py:15
  288.9 2.1 fusion.1
  291.1 4.0 %fusion.5 = bf16[64,4096]{1,0:T(8,128)(2,1)} fusion(bf16[1,4096,256]{2,1,0:T(8,128)(2,1)S(1)} %copy-done, bf16[64,4096]{1,0:T(8,128)(2,1)S(1)} %bitcast.132, bf16[1,4096,256]{2,1,0:T(8,128)(2,1)} %all-gather.5.cloned.1.call-done, bf16[64,4096]{1,0:T(8,128)(2,1)S(1)} %bitcast_multiply_fusion, f32[64,256]{1,0:T(8,128)S(1)} %fusion.15), kind=kOutput, calls=%fused_computation.12 | convolution fusion | flops 269369344 | bytes 5832704 | tf_op jit(solution)/shard_map/dot_general | solution.py:71
  295.1 66.5 %reduce-scatter.2.cloned.1.call-done = bf16[256,256]{1,0:T(8,128)(2,1)} async-done(((bf16[4096,256]{1,0:T(8,128)(2,1)}), bf16[256,256]{1,0:T(8,128)(2,1)}) %reduce-scatter.2.cloned.1.call-update) | async-done | bytes 131088 | tf_op jit(solution)/shard_map/reduce_scatter | solution.py:92
  (67 shorter events, 37.0 us)
Async XLA Ops:
  7.2 8.9 %copy-start.2 = (bf16[1,1,4,2,32,4096]{5,4,3,2,1,0:T(8,128)(2,1)S(1)}, bf16[1,1,4,2,32,4096]{5,4,3,2,1,0:T(8,128)(2,1)}, u32[]{:S(2)}) copy-start(bf16[1,1,4,2,32,4096]{5,4,3,2,1,0:T(8,128)(2,1)} %param.7) | copy-start | bytes 6291460
  7.2 80.5 %all-gather.3.cloned.1.call-start = ((), (), s32[]{:S(2)}) async-start(), calls=%async_computation.1 | async-start | bytes 2228224 | tf_op jit(solution)/shard_map/all_gather | solution.py:45
  7.9 151.9 %all-gather.5.cloned.1.call-start = ((), (), s32[]{:S(2)}) async-start(), calls=%async_computation.2 | async-start | bytes 2228224 | tf_op jit(solution)/shard_map/all_gather | solution.py:46
  8.7 353.0 %reduce-scatter.2.cloned.1.call-start = ((), (), s32[]{:S(2)}) async-start(), calls=%async_computation.3 | async-start | bytes 2228224 | tf_op jit(solution)/shard_map/reduce_scatter | solution.py:92
  87.6 72.2 %copy-start = (bf16[1,4096,256]{2,1,0:T(8,128)(2,1)S(1)}, bf16[1,4096,256]{2,1,0:T(8,128)(2,1)}, u32[]{:S(2)}) copy-start(bf16[1,4096,256]{2,1,0:T(8,128)(2,1)} %all-gather.3.cloned.1.call-done) | copy-start | bytes 6291460
  163.3 9.5 %collective-permute-start.1 = (bf16[1,32,4096]{2,1,0:T(8,128)(2,1)S(1)}, bf16[1,32,4096]{2,1,0:T(8,128)(2,1)S(1)}, u32[]{:S(2)}, u32[]{:S(2)}) collective-permute-start(bf16[1,32,4096]{2,1,0:T(8,128)(2,1)S(1)} %slice_bitcast_fusion.2), channel_id=1, source_target_pairs={{0,1},{1,2},{2,3},{3,4},{4,5},{5,6},{6,7},{7,8},{8,9},{9,10},{10,1... | collective-permute-start | bytes 786440 | tf_op jit(solution)/shard_map/ppermute | solution.py:15
  167.0 8.3 %collective-permute-start = (bf16[1,32,4096]{2,1,0:T(8,128)(2,1)S(1)}, bf16[1,32,4096]{2,1,0:T(8,128)(2,1)S(1)}, u32[]{:S(2)}, u32[]{:S(2)}) collective-permute-start(bf16[1,32,4096]{2,1,0:T(8,128)(2,1)S(1)} %slice_bitcast_fusion.2), channel_id=1, source_target_pairs={{1,0},{2,1},{3,2},{4,3},{5,4},{6,5},{7,6},{8,7},{9,8},{10,9},{11,1... | collective-permute-start | bytes 786440 | tf_op jit(solution)/shard_map/ppermute | solution.py:18
  175.3 5.8 %collective-permute-start.2 = (bf16[32,4096]{1,0:T(8,128)(2,1)S(1)}, bf16[32,4096]{1,0:T(8,128)(2,1)S(1)}, u32[]{:S(2)}, u32[]{:S(2)}) collective-permute-start(bf16[32,4096]{1,0:T(8,128)(2,1)S(1)} %slice_select_fusion.2), channel_id=1, source_target_pairs={{16,0},{32,16},{48,32},{64,48},{80,64},{96,80},{112,96},{128,112},... | collective-permute-start | bytes 786440 | tf_op jit(solution)/shard_map/ppermute | solution.py:26
  182.1 10.9 %collective-permute-start.4 = (bf16[1,32,4096]{2,1,0:T(8,128)(2,1)S(1)}, bf16[1,32,4096]{2,1,0:T(8,128)(2,1)S(1)}, u32[]{:S(2)}, u32[]{:S(2)}) collective-permute-start(bf16[1,32,4096]{2,1,0:T(8,128)(2,1)S(1)} %fusion.58), channel_id=1, source_target_pairs={{1,0},{2,1},{3,2},{4,3},{5,4},{6,5},{7,6},{8,7},{9,8},{10,9},{11,1... | collective-permute-start | bytes 786440 | tf_op jit(solution)/shard_map/ppermute | solution.py:18
  186.6 12.1 %collective-permute-start.3 = (bf16[1,32,4096]{2,1,0:T(8,128)(2,1)S(1)}, bf16[1,32,4096]{2,1,0:T(8,128)(2,1)S(1)}, u32[]{:S(2)}, u32[]{:S(2)}) collective-permute-start(bf16[1,32,4096]{2,1,0:T(8,128)(2,1)S(1)} %fusion.58), channel_id=1, source_target_pairs={{0,1},{1,2},{2,3},{3,4},{4,5},{5,6},{6,7},{7,8},{8,9},{9,10},{10,1... | collective-permute-start | bytes 786440 | tf_op jit(solution)/shard_map/ppermute | solution.py:15
  199.8 14.6 %copy-start.4 = (s32[16]{0:T(128)S(1)}, s32[16]{0:T(128)}, u32[]{:S(2)}) copy-start(s32[16]{0:T(128)} %param.13) | copy-start | bytes 196
  205.7 14.7 %collective-permute-start.6 = (bf16[1,32,4096]{2,1,0:T(8,128)(2,1)}, bf16[1,32,4096]{2,1,0:T(8,128)(2,1)S(1)}, u32[]{:S(2)}, u32[]{:S(2)}) collective-permute-start(bf16[1,32,4096]{2,1,0:T(8,128)(2,1)} %slice_bitcast_fusion.1), channel_id=1, source_target_pairs={{0,1},{1,2},{2,3},{3,4},{4,5},{5,6},{6,7},{7,8},{8,9},{9,10},{10,1... | collective-permute-start | bytes 786440 | tf_op jit(solution)/shard_map/ppermute | solution.py:15
  207.6 12.7 %collective-permute-start.5 = (bf16[1,32,4096]{2,1,0:T(8,128)(2,1)}, bf16[1,32,4096]{2,1,0:T(8,128)(2,1)}, u32[]{:S(2)}, u32[]{:S(2)}) collective-permute-start(bf16[1,32,4096]{2,1,0:T(8,128)(2,1)} %slice_bitcast_fusion.1), channel_id=1, source_target_pairs={{1,0},{2,1},{3,2},{4,3},{5,4},{6,5},{7,6},{8,7},{9,8},{10,9},{11,1... | collective-permute-start | bytes 786440 | tf_op jit(solution)/shard_map/ppermute | solution.py:18
  221.3 12.8 %copy-start.3 = (bf16[1,1,1,2,32,4096]{5,4,3,2,1,0:T(8,128)(2,1)S(1)}, bf16[1,1,1,2,32,4096]{5,4,3,2,1,0:T(8,128)(2,1)}, u32[]{:S(2)}) copy-start(bf16[1,1,1,2,32,4096]{5,4,3,2,1,0:T(8,128)(2,1)} %get-tuple-element.5) | copy-start | bytes 1572868
  221.3 5.9 %collective-permute-start.7 = (bf16[32,4096]{1,0:T(8,128)(2,1)S(1)}, bf16[32,4096]{1,0:T(8,128)(2,1)S(1)}, u32[]{:S(2)}, u32[]{:S(2)}) collective-permute-start(bf16[32,4096]{1,0:T(8,128)(2,1)S(1)} %slice_select_fusion.1), channel_id=1, source_target_pairs={{16,0},{32,16},{48,32},{64,48},{80,64},{96,80},{112,96},{128,112},... | collective-permute-start | bytes 786440 | tf_op jit(solution)/shard_map/ppermute | solution.py:26
  228.2 10.7 %collective-permute-start.9 = (bf16[1,32,4096]{2,1,0:T(8,128)(2,1)S(1)}, bf16[1,32,4096]{2,1,0:T(8,128)(2,1)S(1)}, u32[]{:S(2)}, u32[]{:S(2)}) collective-permute-start(bf16[1,32,4096]{2,1,0:T(8,128)(2,1)S(1)} %fusion.59), channel_id=1, source_target_pairs={{1,0},{2,1},{3,2},{4,3},{5,4},{6,5},{7,6},{8,7},{9,8},{10,9},{11,1... | collective-permute-start | bytes 786440 | tf_op jit(solution)/shard_map/ppermute | solution.py:18
  232.1 12.2 %collective-permute-start.8 = (bf16[1,32,4096]{2,1,0:T(8,128)(2,1)S(1)}, bf16[1,32,4096]{2,1,0:T(8,128)(2,1)S(1)}, u32[]{:S(2)}, u32[]{:S(2)}) collective-permute-start(bf16[1,32,4096]{2,1,0:T(8,128)(2,1)S(1)} %fusion.59), channel_id=1, source_target_pairs={{0,1},{1,2},{2,3},{3,4},{4,5},{5,6},{6,7},{7,8},{8,9},{9,10},{10,1... | collective-permute-start | bytes 786440 | tf_op jit(solution)/shard_map/ppermute | solution.py:15
  249.5 16.8 %copy-start.1 = (f32[4096,256]{1,0:T(8,128)S(1)}, f32[4096,256]{1,0:T(8,128)}, u32[]{:S(2)}) copy-start(f32[4096,256]{1,0:T(8,128)} %fusion.78) | copy-start | bytes 12582916
  250.7 11.6 %collective-permute-start.11 = (bf16[1,32,4096]{2,1,0:T(8,128)(2,1)S(1)}, bf16[1,32,4096]{2,1,0:T(8,128)(2,1)S(1)}, u32[]{:S(2)}, u32[]{:S(2)}) collective-permute-start(bf16[1,32,4096]{2,1,0:T(8,128)(2,1)S(1)} %slice_bitcast_fusion), channel_id=1, source_target_pairs={{0,1},{1,2},{2,3},{3,4},{4,5},{5,6},{6,7},{7,8},{8,9},{9,10},{10,1... | collective-permute-start | bytes 786440 | tf_op jit(solution)/shard_map/ppermute | solution.py:15
  252.7 10.7 %collective-permute-start.10 = (bf16[1,32,4096]{2,1,0:T(8,128)(2,1)S(1)}, bf16[1,32,4096]{2,1,0:T(8,128)(2,1)S(1)}, u32[]{:S(2)}, u32[]{:S(2)}) collective-permute-start(bf16[1,32,4096]{2,1,0:T(8,128)(2,1)S(1)} %slice_bitcast_fusion), channel_id=1, source_target_pairs={{1,0},{2,1},{3,2},{4,3},{5,4},{6,5},{7,6},{8,7},{9,8},{10,9},{11,1... | collective-permute-start | bytes 786440 | tf_op jit(solution)/shard_map/ppermute | solution.py:18
  264.4 5.8 %collective-permute-start.12 = (bf16[32,4096]{1,0:T(8,128)(2,1)S(1)}, bf16[32,4096]{1,0:T(8,128)(2,1)S(1)}, u32[]{:S(2)}, u32[]{:S(2)}) collective-permute-start(bf16[32,4096]{1,0:T(8,128)(2,1)S(1)} %slice_select_fusion), channel_id=1, source_target_pairs={{16,0},{32,16},{48,32},{64,48},{80,64},{96,80},{112,96},{128,112},... | collective-permute-start | bytes 786440 | tf_op jit(solution)/shard_map/ppermute | solution.py:26
  271.2 12.2 %collective-permute-start.14 = (bf16[1,32,4096]{2,1,0:T(8,128)(2,1)S(1)}, bf16[1,32,4096]{2,1,0:T(8,128)(2,1)S(1)}, u32[]{:S(2)}, u32[]{:S(2)}) collective-permute-start(bf16[1,32,4096]{2,1,0:T(8,128)(2,1)S(1)} %fusion.60), channel_id=1, source_target_pairs={{1,0},{2,1},{3,2},{4,3},{5,4},{6,5},{7,6},{8,7},{9,8},{10,9},{11,1... | collective-permute-start | bytes 786440 | tf_op jit(solution)/shard_map/ppermute | solution.py:18
  276.8 11.9 %collective-permute-start.13 = (bf16[1,32,4096]{2,1,0:T(8,128)(2,1)S(1)}, bf16[1,32,4096]{2,1,0:T(8,128)(2,1)S(1)}, u32[]{:S(2)}, u32[]{:S(2)}) collective-permute-start(bf16[1,32,4096]{2,1,0:T(8,128)(2,1)S(1)} %fusion.60), channel_id=1, source_target_pairs={{0,1},{1,2},{2,3},{3,4},{4,5},{5,6},{6,7},{7,8},{8,9},{9,10},{10,1... | collective-permute-start | bytes 786440 | tf_op jit(solution)/shard_map/ppermute | solution.py:15
Sparse Core Ops, SparseCore 0:
  10.1 77.5 all-gather.2
  89.7 70.0 all-gather.4
  291.2 70.3 reduce-scatter.1
where the time goes:
time: 371 us; the launch traced here: 370 us
  waiting for transfers between devices  250 us (67%)
  starting transfers between devices  47.1 us (13%)
  matrix products  27.8 us (7%)
  between operations  23.8 us (6%)
  other arithmetic  12.3 us (3%)
  local copies, waits for them, and re-layouts  8.34 us (2%)
    all_gather x1, waiting for transfers between devices, body(): lax.all_gather(down_weight, 'dp', axis=1, tiled=True)  70.4 us
    all_gather x1, waiting for transfers between devices, body(): lax.all_gather(up_weight, 'dp', axis=1, tiled=True)  70 us
    reduce_scatter x1, waiting for transfers between devices, body(): lax.psum_scatter(partial_value.astype(jnp.bfloat16), 'dp', scatter_dimens...  66.5 us
    ppermute x6, starting transfers between devices, extended(): lax.ppermute(lax.slice_in_dim(block, 0, width, axis=dim), axis, backward)  27.6 us
    ppermute x6, waiting for transfers between devices, extended(): lax.ppermute(lax.slice_in_dim(block, block.shape[dim] - width, None, axis...  21.1 us
    dot_general x4, matrix products, body(): lax.dot_general(inner_grad, w_down, (((1,), (1,)), ((), ())), preferred_e...  15.8 us
    ppermute x6, waiting for transfers between devices, extended(): lax.ppermute(lax.slice_in_dim(block, 0, width, axis=dim), axis, backward)  14.7 us
    ppermute x6, starting transfers between devices, extended(): lax.ppermute(lax.slice_in_dim(block, block.shape[dim] - width, None, axis...  13.5 us
  transfers between devices with their start and end apart: 18, of which 16 were waited for; matrix products, arithmetic and copies ran while one was open for 6% of the time, Pallas kernels for 0%

commit v1 on v0

v1 whole, which is shorter than its diff:
```python
import functools
import math

import jax
import jax.numpy as jnp
from jax import lax
from jax.experimental import pallas as pl
from jax.experimental.pallas import tpu as pltpu
from jax.sharding import PartitionSpec as P

MESH = pl.DeviceIdType.MESH
F32, BF16 = jnp.float32, jnp.bfloat16
RIGHT, LEFT = 0, 1
INC, HID, LEAVE = 0, 1, 2


def kernel(S, N, K, T, D, R, NC,
           saved, incoming, head, wd, wu, adopt, live, leaving, grad,
           wdf, wuf, x, inc, inc_in, hacc, h_in, cacc, g, u, fac, outb, leave_in, rs_out, rs_in, plan,
           lsem, ws, wr, xs, xr, cs, cr, rss, rsr):
    H, blk = N // 2, D // N
    half, rows = blk // 2, K * T
    cols = D // NC
    per = cols // blk
    sec, me = lax.axis_index("section"), lax.axis_index("dp")
    right, left = lax.rem(me + 1, N), lax.rem(me + N - 1, N)
    below, above = lax.rem(sec + S - 1, S), lax.rem(sec + 1, S)
    side = ((sec, right), (sec, left))

    loads = [
        pltpu.make_async_copy(wd.at[0], wdf.at[me], lsem.at[0]),
        pltpu.make_async_copy(wu.at[0], wuf.at[me], lsem.at[1]),
        pltpu.make_async_copy(incoming.at[0, 0], inc, lsem.at[2]),
        pltpu.make_async_copy(adopt, plan, lsem.at[3]),
        pltpu.make_async_copy(saved.at[0, 0, :, 0], x.at[0], lsem.at[4]),
        pltpu.make_async_copy(saved.at[0, 0, :, 1], x.at[1], lsem.at[5]),
    ]
    for load in loads:
        load.start()
    heads = [pltpu.make_async_copy(head.at[k, 0], g.at[k + 1], lsem.at[6 + k]) for k in range(K - 1)]

    @pl.when(sec == S - 1)
    def _():
        for load in heads:
            load.start()

    barrier = pltpu.get_barrier_semaphore()
    for target in ((sec, left), (sec, right), (below, me), (above, me)):
        pl.semaphore_signal(barrier, inc=1, device_id=target, device_id_type=MESH)
    pl.semaphore_wait(barrier, 4)

    def remote(src, dst, send, recv, target):
        return pltpu.make_async_remote_copy(
            src_ref=src, dst_ref=dst, send_sem=send, recv_sem=recv, device_id=target, device_id_type=MESH
        )

    full = (wdf, wuf)

    def away(way, distance):
        return lax.rem(me + N - distance, N) if way == RIGHT else lax.rem(me + distance, N)

    def weight(w, way, hop, c, arriving):
        owner = away(way, hop if arriving else hop - 1)
        ref = full[w].at[owner, pl.ds(c * half, half)]
        return remote(ref, ref, ws.at[w, way, hop - 1, c], wr.at[w, way, hop - 1, c], side[way])

    def exchange(e, way, src, dst):
        return remote(src, dst.at[way], xs.at[e, way], xr.at[e, way], side[way])

    def add_h(b):
        columns = pl.ds(pl.multiple_of(b * blk, blk), blk)
        block = x[:, :, :, columns].reshape(2 * rows, blk)
        hacc[...] += jnp.dot(block, wdf[b], preferred_element_type=F32)

    def add_c(b):
        columns = pl.ds(pl.multiple_of(b * blk, blk), blk)
        cacc[...] += jnp.dot(g[0, :, columns], wuf[b], preferred_element_type=F32)

    def hops(w, add):
        def step(hop, _):
            for c in (0, 1):
                for way in (RIGHT, LEFT):
                    weight(w, way, hop - 1, c, True).wait_recv()
                    weight(w, way, hop, c, False).start()
            add(away(RIGHT, hop - 1))
            add(away(LEFT, hop - 1))
            return 0

        lax.fori_loop(2, H, step, 0)
        for c in (0, 1):
            for way in (RIGHT, LEFT):
                weight(w, way, H - 1, c, True).wait_recv()
                if c == way:
                    weight(w, way, H, c, False).start()

    def last_hop(w, add):
        add(away(RIGHT, H - 1))
        add(away(LEFT, H - 1))
        for way in (RIGHT, LEFT):
            weight(w, way, H, way, True).wait_recv()
        add(away(RIGHT, H))

    def first_hop(w):
        for c in (0, 1):
            for way in (RIGHT, LEFT):
                weight(w, way, 1, c, False).start()

    loads[0].wait()
    first_hop(0)
    loads[2].wait()
    inc_copies = [exchange(INC, way, inc.at[1], inc_in) for way in (RIGHT, LEFT)]
    for copy in inc_copies:
        copy.start()
    loads[1].wait()
    loads[3].wait()
    loads[4].wait()
    loads[5].wait()
    hacc[...] = jnp.zeros_like(hacc)
    add_h(me)
    hops(0, add_h)
    first_hop(1)
    last_hop(0, add_h)
    hid_copies = [exchange(HID, way, hacc.at[pl.ds(rows, rows)], h_in) for way in (RIGHT, LEFT)]
    for copy in hid_copies:
        copy.start()

    for copy in inc_copies:
        copy.wait_recv()
    offsets = [plan[me, k, sec] for k in range(K)]
    first = offsets[0]
    g[0] = jnp.where(first == 0, inc[0], jnp.where(first == 1, inc_in[LEFT], inc_in[RIGHT]))
    cacc[...] = jnp.zeros_like(cacc)
    add_c(me)
    hops(1, add_c)
    for copy in hid_copies:
        copy.wait_recv()
    for k in range(K):
        d = offsets[k]
        part = pl.ds(k * T, T)
        h = jnp.where(d == 0, hacc[part], jnp.where(d == 1, h_in[LEFT, part], h_in[RIGHT, part]))
        gate = jax.nn.sigmoid(h)
        fac[k] = gate * (1.0 + h * (1.0 - gate))
        joins = jnp.where(d == 0, live[me], jnp.where(d == 1, live[right], live[left]))
        u[part] = jnp.where(joins == 1, h * gate, 0.0).astype(BF16)
    last_hop(1, add_c)

    def chain(k, j):
        part = pl.ds(j * cols, cols)
        return remote(outb.at[k, :, part], g.at[k + 1, :, part], cs.at[k, j], cr.at[k, j], (below, me))

    def out_chunk(k, j, inner):
        part = pl.ds(j * cols, cols)
        back = lax.dot_general(
            inner, wdf[pl.ds(j * per, per)].reshape(cols, R), (((1,), (1,)), ((), ())), preferred_element_type=F32
        )
        outb[k, :, part] = (g[k, :, part].astype(F32) + back).astype(BF16)

    @pl.when(sec == S - 1)
    def _():
        for load in heads:
            load.wait()

    for k in range(K - 1):
        inner = (fac[k] * cacc[...]).astype(BF16)
        for j in range(NC):
            out_chunk(k, j, inner)

            @pl.when(sec > 0)
            def _():
                chain(k, j).start()

        total = jnp.zeros((T, R), F32)
        for j in range(NC):
            @pl.when(sec < S - 1)
            def _():
                chain(k, j).wait_recv()

            total += jnp.dot(
                g[k + 1, :, pl.ds(j * cols, cols)], wuf[pl.ds(j * per, per)].reshape(cols, R),
                preferred_element_type=F32,
            )
        cacc[...] = total

    def own(r):
        columns = pl.ds(pl.multiple_of(r * blk, blk), blk)
        return lax.dot_general(
            g[:, :, columns].reshape(rows, blk), u[...], (((0,), (0,)), ((), ())), preferred_element_type=F32
        )

    def ring_sum(way, step, c):
        part = pl.ds(c * half, half)
        return remote(
            rs_out.at[way, step - 1, part], rs_in.at[way, step - 1, part],
            rss.at[way, step - 1, c], rsr.at[way, step - 1, c], side[way],
        )

    def target(way, step):
        return away(1 - way, H + 1 - step)

    term = own(target(RIGHT, 1))
    for way in (RIGHT, LEFT):
        rs_out[way, 0, pl.ds(way * half, half)] = term[way * half : (way + 1) * half].astype(BF16)
        ring_sum(way, 1, way).start()

    inner = (fac[K - 1] * cacc[...]).astype(BF16)
    for j in range(NC):
        out_chunk(K - 1, j, inner)
    leave_copies = [exchange(LEAVE, way, outb.at[K - 1], leave_in) for way in (RIGHT, LEFT)]
    for copy in leave_copies:
        copy.start()

    for way in (RIGHT, LEFT):
        term = own(target(way, 2))
        for c in (way, 1 - way):
            part = pl.ds(c * half, half)
            value = term[c * half : (c + 1) * half]
            if c == way:
                ring_sum(way, 1, c).wait_recv()
                value = value + rs_in[way, 0, part].astype(F32)
            rs_out[way, 1, part] = value.astype(BF16)
            ring_sum(way, 2, c).start()

    def sum_step(step, _):
        terms = [own(target(way, step)) for way in (RIGHT, LEFT)]
        for c in (0, 1):
            part = pl.ds(c * half, half)
            for way in (RIGHT, LEFT):
                ring_sum(way, step - 1, c).wait_recv()
                value = terms[way][c * half : (c + 1) * half] + rs_in[way, step - 2, part].astype(F32)
                rs_out[way, step - 1, part] = value.astype(BF16)
                ring_sum(way, step, c).start()
        return 0

    lax.fori_loop(3, H + 1, sum_step, 0)

    last = offsets[K - 1]
    leaving[0, 0, 0] = jnp.where(last == 0, outb[K - 1], jnp.zeros((T, D), BF16))
    for copy in leave_copies:
        copy.wait_recv()
    leaving[0, 0, 1] = jnp.where(
        plan[left, K - 1, sec] == 1,
        leave_in[RIGHT],
        jnp.where(plan[right, K - 1, sec] == -1, leave_in[LEFT], jnp.zeros((T, D), BF16)),
    )

    scale = 1.0 / math.sqrt(N * K * T)
    term = own(me)
    for c in (0, 1):
        part = pl.ds(c * half, half)
        for way in (RIGHT, LEFT):
            ring_sum(way, H, c).wait_recv()
        total = term[c * half : (c + 1) * half]
        total = total + rs_in[RIGHT, H - 1, part].astype(F32) + rs_in[LEFT, H - 1, part].astype(F32)
        grad[0, part] = (total * scale).astype(BF16)

    def drain_weights(hop, _):
        for w in (0, 1):
            for way in (RIGHT, LEFT):
                for c in (0, 1):
                    weight(w, way, hop, c, False).wait_send()
        return 0

    lax.fori_loop(1, H, drain_weights, 0)
    for w in (0, 1):
        for way in (RIGHT, LEFT):
            weight(w, way, H, way, False).wait_send()
    for copy in inc_copies + hid_copies + leave_copies:
        copy.wait_send()

    @pl.when(sec > 0)
    def _():
        for k in range(K - 1):
            for j in range(NC):
                chain(k, j).wait_send()

    for way in (RIGHT, LEFT):
        ring_sum(way, 1, way).wait_send()

    def drain_sums(step, _):
        for way in (RIGHT, LEFT):
            for c in (0, 1):
                ring_sum(way, step, c).wait_send()
        return 0

    lax.fori_loop(2, H + 1, drain_sums, 0)


def solution(mesh):
    S, N = mesh.shape["section"], mesh.shape["dp"]

    def body(saved, incoming, head, wd, wu, adopt, live):
        _, _, K, _, T, D = saved.shape
        blk, R = wd.shape[1:]
        H, rows, NC = N // 2, K * T, 4
        anywhere = pl.BlockSpec(memory_space=pl.ANY)
        vmem = pl.BlockSpec(memory_space=pltpu.VMEM)
        dma = pltpu.SemaphoreType.DMA
        return pl.pallas_call(
            functools.partial(kernel, S, N, K, T, D, R, NC),
            out_shape=(
                jax.ShapeDtypeStruct((1, 1, 2, T, D), BF16),
                jax.ShapeDtypeStruct((1, blk, R), BF16),
            ),
            in_specs=[anywhere] * 6 + [pl.BlockSpec(memory_space=pltpu.SMEM)],
            out_specs=(vmem, vmem),
            scratch_shapes=[
                pltpu.VMEM((N, blk, R), BF16),
                pltpu.VMEM((N, blk, R), BF16),
                pltpu.VMEM((2, K, T, D), BF16),
                pltpu.VMEM((2, T, D), BF16),
                pltpu.VMEM((2, T, D), BF16),
                pltpu.VMEM((2 * rows, R), F32),
                pltpu.VMEM((2, rows, R), F32),
                pltpu.VMEM((T, R), F32),
                pltpu.VMEM((K, T, D), BF16),
                pltpu.VMEM((rows, R), BF16),
                pltpu.VMEM((K, T, R), F32),
                pltpu.VMEM((K, T, D), BF16),
                pltpu.VMEM((2, T, D), BF16),
                pltpu.VMEM((2, H, blk, R), BF16),
                pltpu.VMEM((2, H, blk, R), BF16),
                pltpu.SMEM((N, K, S), jnp.int32),
                dma((5 + K,)),
                dma((2, 2, H, 2)),
                dma((2, 2, H, 2)),
                dma((3, 2)),
                dma((3, 2)),
                dma((K - 1, NC)),
                dma((K - 1, NC)),
                dma((2, H, 2)),
                dma((2, H, 2)),
            ],
            compiler_params=pltpu.CompilerParams(
                collective_id=0, has_side_effects=True, vmem_limit_bytes=40 * 1024 * 1024
            ),
        )(saved, incoming, head, wd, wu, adopt.transpose(1, 2, 0), live)

    return jax.shard_map(
        body,
        mesh=mesh,
        in_specs=(
            P("section", "dp", None, None, None, None),
            P("section", "dp", None, None, None),
            P(None, "dp", None, None),
            P("section", "dp", None),
            P("section", "dp", None),
            P(),
            P(),
        ),
        out_specs=(P("section", "dp", None, None, None), P("section", "dp", None)),
        check_vma=False,
    )
```

time: 371 us -> 139 us (0.37)
  the two profiles are of different devices: /device:TPU:4 before, /device:TPU:1 now
where the time goes in v1:
time: 139 us; the launch traced here: 137 us
  Pallas kernels  128 us (92%)
  local copies, waits for them, and re-layouts  8.43 us (6%)
    pallas_call x1, Pallas kernels, body(): pl.pallas_call(functools.partial(kernel, S, N, K, T, D, R, NC), out_shape...  128 us
    unnamed x16, local copies, waits for them, and re-layouts  8.43 us

profile of v1, /device:TPU:1, one launch (start us, length us, event | category | flops | bytes accessed | tf_op | source)
XLA Modules:
  0.0 136.6 jit_solution(13072730025560232960)
XLA Ops:
  0.6 0.0 copy-start
  0.6 1.6 %copy-done = bf16[1,1,4,2,32,4096]{5,4,3,2,1,0:T(8,128)(2,1)S(1)} copy-done((bf16[1,1,4,2,32,4096]{5,4,3,2,1,0:T(8,128)(2,1)S(1)}, bf16[1,1,4,2,32,4096]{5,4,3,2,1,0:T(8,128)(2,1)}, u32[]{:S(2)}) %copy-start) | copy-done | bytes 2097176
  2.2 0.0 copy-start.1
  2.2 1.1 copy-done.1
  3.4 0.0 copy-start.2
  3.4 1.0 copy-done.2
  4.4 0.0 copy-start.3
  4.4 0.9 copy-done.3
  5.3 0.0 copy-start.4
  5.3 0.9 copy-done.4
  6.2 0.0 copy-start.5
  6.2 0.8 copy-done.5
  7.0 0.0 copy-start.6
  7.0 0.7 copy-done.6
  7.6 127.5 %shard_map.86 = (bf16[1,1,2,32,4096]{4,3,2,1,0:T(8,128)(2,1)S(1)}, bf16[1,256,256]{2,1,0:T(8,128)(2,1)S(1)}) custom-call(bf16[1,1,4,2,32,4096]{5,4,3,2,1,0:T(8,128)(2,1)S(1)} %copy-done, bf16[1,1,2,32,4096]{4,3,2,1,0:T(8,128)(2,1)S(1)} %copy-done.2, bf16[3,1,32,4096]{3,2,1,0:T(8,128)(2,1)S(1)} %copy-done.1, bf16[1,256,256]{2,1,0:T(8,128)(2,1)S(1)} %copy-done.3, ...), custom_call_target="tpu_custom_call" | custom-call | tf_op jit(solution)/shard_map/pallas_call | solution.py:298
  135.2 0.8 copy.11
  136.0 0.7 copy.12
Async XLA Ops:
  0.6 1.6 %copy-start = (bf16[1,1,4,2,32,4096]{5,4,3,2,1,0:T(8,128)(2,1)S(1)}, bf16[1,1,4,2,32,4096]{5,4,3,2,1,0:T(8,128)(2,1)}, u32[]{:S(2)}) copy-start(bf16[1,1,4,2,32,4096]{5,4,3,2,1,0:T(8,128)(2,1)} %saved.1) | copy-start | bytes 6291460
  2.2 1.1 copy-start.1
  3.4 1.0 copy-start.2
  4.4 0.9 copy-start.3
  5.3 0.9 copy-start.4
  6.2 0.8 copy-start.5
  7.0 0.7 copy-start.6

commit v2 on v1

v2 whole, which is shorter than its diff:
```python
import functools
import math

import jax
import jax.numpy as jnp
from jax import lax
from jax.experimental import pallas as pl
from jax.experimental.pallas import tpu as pltpu
from jax.sharding import PartitionSpec as P

MESH = pl.DeviceIdType.MESH
F32, BF16 = jnp.float32, jnp.bfloat16
RIGHT, LEFT = 0, 1
INC, HID, LEAVE = 0, 1, 2
DOWN, UP = 0, 1


def kernel(S, N, K, T, D, R,
           saved, incoming, head, wd, wu, adopt, live, leaving, grad,
           wdf, wuf, x, inc, inc_in, hacc, hb, h_in, cacc, g, u, fac, outb, leave_in, rs_out, rs_in, plan,
           lsem, ws, wr, xs, xr, cs, cr, rss, rsr):
    H, blk = N // 2, D // N
    half, rows = blk // 2, K * T
    sec, me = lax.axis_index("section"), lax.axis_index("dp")
    right, left = lax.rem(me + 1, N), lax.rem(me + N - 1, N)
    below, above = lax.rem(sec + S - 1, S), lax.rem(sec + 1, S)
    side = ((sec, right), (sec, left))

    loads = [
        pltpu.make_async_copy(wd.at[0], wdf.at[me], lsem.at[0]),
        pltpu.make_async_copy(wu.at[0], wuf.at[me], lsem.at[1]),
        pltpu.make_async_copy(incoming.at[0, 0], inc, lsem.at[2]),
        pltpu.make_async_copy(adopt, plan, lsem.at[3]),
        pltpu.make_async_copy(saved.at[0, 0, :, 0], x.at[0], lsem.at[4]),
        pltpu.make_async_copy(saved.at[0, 0, :, 1], x.at[1], lsem.at[5]),
    ]
    for load in loads:
        load.start()
    heads = [pltpu.make_async_copy(head.at[k, 0], g.at[k + 1], lsem.at[6 + k]) for k in range(K - 1)]

    @pl.when(sec == S - 1)
    def _():
        for load in heads:
            load.start()

    barrier = pltpu.get_barrier_semaphore()
    for target in ((sec, left), (sec, right), (below, me), (above, me)):
        pl.semaphore_signal(barrier, inc=1, device_id=target, device_id_type=MESH)
    pl.semaphore_wait(barrier, 4)

    def remote(src, dst, send, recv, target):
        return pltpu.make_async_remote_copy(
            src_ref=src, dst_ref=dst, send_sem=send, recv_sem=recv, device_id=target, device_id_type=MESH
        )

    full = (wdf, wuf)

    def away(way, distance):
        return lax.rem(me + N - distance, N) if way == RIGHT else lax.rem(me + distance, N)

    def weight(w, way, hop, arriving):
        ref = full[w].at[away(way, hop if arriving else hop - 1)]
        if isinstance(hop, int) and hop == H:
            ref = ref.at[pl.ds(way * half, half)]
        return remote(ref, ref, ws.at[w, way, hop - 1], wr.at[w, way, hop - 1], side[way])

    def exchange(e, way, src, dst):
        return remote(src, dst.at[way], xs.at[e, way], xr.at[e, way], side[way])

    def block(b):
        return pl.ds(pl.multiple_of(b * blk, blk), blk)

    def add_h(b):
        inputs = x[:, :, :, block(b)].reshape(2 * rows, blk)
        hacc[...] += jnp.dot(inputs, wdf[b], preferred_element_type=F32)

    def add_c(b):
        cacc[...] += jnp.dot(g[0, :, block(b)], wuf[b], preferred_element_type=F32)

    def pass_on(w, hop):
        for way in (RIGHT, LEFT):
            if hop > 1:
                weight(w, way, hop - 1, True).wait_recv()
            if hop <= H:
                weight(w, way, hop, False).start()

    def add_blocks(w, hop):
        add = (add_h, add_c)[w]
        for way in (RIGHT, LEFT) if 1 < hop <= H else (RIGHT,):
            add(away(way, hop - 1))

    loads[0].wait()
    pass_on(DOWN, 1)
    loads[2].wait()
    inc_copies = [exchange(INC, way, inc.at[1], inc_in) for way in (RIGHT, LEFT)]
    for copy in inc_copies:
        copy.start()
    for load in (loads[1], loads[3], loads[4], loads[5]):
        load.wait()
    offsets = [plan[me, k, sec] for k in range(K)]
    hacc[...] = jnp.zeros_like(hacc)
    cacc[...] = jnp.zeros_like(cacc)
    add_blocks(DOWN, 1)
    for hop in range(2, H + 2):
        pass_on(DOWN, hop)
        add_blocks(DOWN, hop)
        if hop == 2:
            for copy in inc_copies:
                copy.wait_recv()
        if hop == H + 1:
            hb[...] = hacc[pl.ds(rows, rows)].astype(BF16)
            hid_copies = [exchange(HID, way, hb, h_in) for way in (RIGHT, LEFT)]
            for copy in hid_copies:
                copy.start()
        pass_on(UP, hop - 1)
        if hop == 2:
            d = offsets[0]
            g[0] = jnp.where(d == 0, inc[0], jnp.where(d == 1, inc_in[LEFT], inc_in[RIGHT]))
        add_blocks(UP, hop - 1)

    for copy in hid_copies:
        copy.wait_recv()
    for k in range(K):
        d = offsets[k]
        part = pl.ds(k * T, T)
        h = jnp.where(d == 0, hacc[part], jnp.where(d == 1, h_in[LEFT, part], h_in[RIGHT, part]).astype(F32))
        gate = jax.nn.sigmoid(h)
        fac[k] = gate * (1.0 + h * (1.0 - gate))
        joins = jnp.where(d == 0, live[me], jnp.where(d == 1, live[right], live[left]))
        u[part] = jnp.where(joins == 1, h * gate, 0.0).astype(BF16)
    pass_on(UP, H + 1)
    add_blocks(UP, H + 1)

    ring = [away(RIGHT, H)]
    for distance in range(H - 1, 0, -1):
        ring += [away(LEFT, distance), away(RIGHT, distance)]
    ring.append(me)

    def chain(k, i):
        part = block(ring[i])
        return remote(outb.at[k, :, part], g.at[k + 1, :, part], cs.at[k, i], cr.at[k, i], (below, me))

    def out_block(k, i, inner):
        part = block(ring[i])
        back = lax.dot_general(inner, wdf[ring[i]], (((1,), (1,)), ((), ())), preferred_element_type=F32)
        outb[k, :, part] = (g[k, :, part].astype(F32) + back).astype(BF16)

    def next_c(k, i):
        @pl.when(sec < S - 1)
        def _():
            chain(k, i).wait_recv()

        return jnp.dot(g[k + 1, :, block(ring[i])], wuf[ring[i]], preferred_element_type=F32)

    @pl.when(sec == S - 1)
    def _():
        for load in heads:
            load.wait()

    def send_out(k):
        inner = (fac[k] * cacc[...]).astype(BF16)
        for i in range(N):
            out_block(k, i, inner)

            @pl.when(sec > 0)
            def _():
                chain(k, i).start()

    for k in range(K - 2):
        send_out(k)
        total = next_c(k, 0)
        for i in range(1, N):
            total += next_c(k, i)
        cacc[...] = total

    def own(r, c):
        columns = pl.ds(pl.multiple_of(r * blk + c * half, half), half)
        return lax.dot_general(
            g[:, :, columns].reshape(rows, half), u[...], (((0,), (0,)), ((), ())), preferred_element_type=F32
        )

    def ring_sum(way, step, c):
        part = pl.ds(c * half, half)
        return remote(
            rs_out.at[way, step - 1, part], rs_in.at[way, step - 1, part],
            rss.at[way, step - 1, c], rsr.at[way, step - 1, c], side[way],
        )

    def sum_step(stream, step, fresh=False):
        pairs = [(way, way ^ stream) for way in (RIGHT, LEFT)]
        terms = [own(away(1 - way, H + 1 - step), c) for way, c in pairs]
        for (way, c), value in zip(pairs, terms):
            part = pl.ds(c * half, half)
            if not fresh:
                ring_sum(way, step - 1, c).wait_recv()
                value = value + rs_in[way, step - 2, part].astype(F32)
            rs_out[way, step - 1, part] = value.astype(BF16)
            ring_sum(way, step, c).start()

    send_out(K - 2)
    total = next_c(K - 2, 0)
    sum_step(0, 1, fresh=True)
    total += next_c(K - 2, 1)
    total += next_c(K - 2, 2)
    sum_step(1, 2, fresh=True)
    for i in range(3, N):
        total += next_c(K - 2, i)

    inner = (fac[K - 1] * total).astype(BF16)
    for i in range(N):
        out_block(K - 1, i, inner)
    leave_copies = [exchange(LEAVE, way, outb.at[K - 1], leave_in) for way in (RIGHT, LEFT)]
    for copy in leave_copies:
        copy.start()

    def sum_steps(step, _):
        sum_step(0, step)
        sum_step(1, step + 1)
        return 0

    lax.fori_loop(2, H, sum_steps, 0)
    sum_step(0, H)

    last = offsets[K - 1]
    leaving[0, 0, 0] = jnp.where(last == 0, outb[K - 1], jnp.zeros((T, D), BF16))
    for copy in leave_copies:
        copy.wait_recv()
    leaving[0, 0, 1] = jnp.where(
        plan[left, K - 1, sec] == 1,
        leave_in[RIGHT],
        jnp.where(plan[right, K - 1, sec] == -1, leave_in[LEFT], jnp.zeros((T, D), BF16)),
    )

    scale = 1.0 / math.sqrt(N * K * T)
    for c in (0, 1):
        part = pl.ds(c * half, half)
        total = own(me, c)
        for way in (RIGHT, LEFT):
            ring_sum(way, H, c).wait_recv()
            total = total + rs_in[way, H - 1, part].astype(F32)
        grad[0, part] = (total * scale).astype(BF16)

    for w in (DOWN, UP):
        for way in (RIGHT, LEFT):
            for hop in range(1, H + 1):
                weight(w, way, hop, False).wait_send()
    for copy in inc_copies + hid_copies + leave_copies:
        copy.wait_send()

    @pl.when(sec > 0)
    def _():
        for k in range(K - 1):
            for i in range(N):
                chain(k, i).wait_send()

    for way in (RIGHT, LEFT):
        ring_sum(way, 1, way).wait_send()

    def drain_sums(step, _):
        for way in (RIGHT, LEFT):
            for c in (0, 1):
                ring_sum(way, step, c).wait_send()
        return 0

    lax.fori_loop(2, H + 1, drain_sums, 0)


def solution(mesh):
    S, N = mesh.shape["section"], mesh.shape["dp"]

    def body(saved, incoming, head, wd, wu, adopt, live):
        _, _, K, _, T, D = saved.shape
        blk, R = wd.shape[1:]
        H, rows = N // 2, K * T
        anywhere = pl.BlockSpec(memory_space=pltpu.HBM)
        vmem = pl.BlockSpec(memory_space=pltpu.VMEM)
        dma = pltpu.SemaphoreType.DMA
        return pl.pallas_call(
            functools.partial(kernel, S, N, K, T, D, R),
            out_shape=(
                jax.ShapeDtypeStruct((1, 1, 2, T, D), BF16),
                jax.ShapeDtypeStruct((1, blk, R), BF16),
            ),
            in_specs=[anywhere] * 6 + [pl.BlockSpec(memory_space=pltpu.SMEM)],
            out_specs=(vmem, vmem),
            scratch_shapes=[
                pltpu.VMEM((N, blk, R), BF16),
                pltpu.VMEM((N, blk, R), BF16),
                pltpu.VMEM((2, K, T, D), BF16),
                pltpu.VMEM((2, T, D), BF16),
                pltpu.VMEM((2, T, D), BF16),
                pltpu.VMEM((2 * rows, R), F32),
                pltpu.VMEM((rows, R), BF16),
                pltpu.VMEM((2, rows, R), BF16),
                pltpu.VMEM((T, R), F32),
                pltpu.VMEM((K, T, D), BF16),
                pltpu.VMEM((rows, R), BF16),
                pltpu.VMEM((K, T, R), F32),
                pltpu.VMEM((K, T, D), BF16),
                pltpu.VMEM((2, T, D), BF16),
                pltpu.VMEM((2, H, blk, R), BF16),
                pltpu.VMEM((2, H, blk, R), BF16),
                pltpu.SMEM((N, K, S), jnp.int32),
                dma((5 + K,)),
                dma((2, 2, H)),
                dma((2, 2, H)),
                dma((3, 2)),
                dma((3, 2)),
                dma((K - 1, N)),
                dma((K - 1, N)),
                dma((2, H, 2)),
                dma((2, H, 2)),
            ],
            compiler_params=pltpu.CompilerParams(
                collective_id=0, has_side_effects=True, vmem_limit_bytes=60 * 1024 * 1024
            ),
        )(saved, incoming, head, wd, wu, adopt.transpose(1, 2, 0), live)

    return jax.shard_map(
        body,
        mesh=mesh,
        in_specs=(
            P("section", "dp", None, None, None, None),
            P("section", "dp", None, None, None),
            P(None, "dp", None, None),
            P("section", "dp", None),
            P("section", "dp", None),
            P(),
            P(),
        ),
        out_specs=(P("section", "dp", None, None, None), P("section", "dp", None)),
        check_vma=False,
    )
```

time: 139 us -> 122 us (0.88)
  the two profiles are of different devices: /device:TPU:1 before, /device:TPU:22 now
where the time goes in v2:
time: 122 us
  Pallas kernels  118 us (97%)
  local copies, waits for them, and re-layouts  3.44 us (3%)
    pallas_call x1, Pallas kernels, body(): pl.pallas_call(functools.partial(kernel, S, N, K, T, D, R), out_shape=(ja...  118 us
    unnamed x2, local copies, waits for them, and re-layouts  3.44 us

profile of v2, /device:TPU:22, one launch (start us, length us, event | category | flops | bytes accessed | tf_op | source)
XLA Modules:
  0.0 122.0 jit_solution(4267802847480026823)
XLA Ops:
  0.6 117.9 %shard_map.86 = (bf16[1,1,2,32,4096]{4,3,2,1,0:T(8,128)(2,1)}, bf16[1,256,256]{2,1,0:T(8,128)(2,1)}) custom-call(bf16[1,1,4,2,32,4096]{5,4,3,2,1,0:T(8,128)(2,1)} %saved.1, bf16[1,1,2,32,4096]{4,3,2,1,0:T(8,128)(2,1)} %incoming.1, bf16[3,1,32,4096]{3,2,1,0:T(8,128)(2,1)} %head.1, bf16[1,256,256]{2,1,0:T(8,128)(2,1)} %wd.1, bf16[1,256,256]{2,1,0:T(8,128)(2,1)} %wu.1, ...), custom_call_target="tpu_custom_call" | custom-call | tf_op jit(solution)/shard_map/pallas_call | solution.py:278
  118.6 1.9 %copy.11 = bf16[1,1,2,32,4096]{4,3,2,1,0:T(8,128)(2,1)} copy(bf16[1,1,2,32,4096]{4,3,2,1,0:T(8,128)(2,1)} %get-tuple-element.4) | data formatting | bytes 1048576
  120.4 1.6 %copy.12 = bf16[1,256,256]{2,1,0:T(8,128)(2,1)} copy(bf16[1,256,256]{2,1,0:T(8,128)(2,1)} %get-tuple-element.5) | data formatting | bytes 262144

commit v3 on v2

v3 whole, which is shorter than its diff:
```python
import functools
import math

import jax
import jax.numpy as jnp
from jax import lax
from jax.experimental import pallas as pl
from jax.experimental.pallas import tpu as pltpu
from jax.sharding import PartitionSpec as P

MESH = pl.DeviceIdType.MESH
F32, BF16 = jnp.float32, jnp.bfloat16
RIGHT, LEFT = 0, 1
INC, HID, LEAVE = 0, 1, 2
DOWN, UP = 0, 1


def kernel(S, N, K, T, D, R,
           saved, incoming, head, wd, wu, adopt, live, leaving, grad,
           wdf, wuf, wda, x, inc, inc_in, hacc, hb, h_in, cacc, g, ga, u, fac, inner_out, inner_in, out, leave_in,
           rs_out, rs_in, plan, lsem, hsem, ws, wr, ds, dr, xs, xr, gs, gr, ns, nr, cs, cr, rss, rsr):
    H, blk = N // 2, D // N
    half, rows = blk // 2, K * T
    sec, me = lax.axis_index("section"), lax.axis_index("dp")
    right, left = lax.rem(me + 1, N), lax.rem(me + N - 1, N)
    below, above = lax.rem(sec + S - 1, S), lax.rem(sec + 1, S)
    side = ((sec, right), (sec, left))

    offset = [H] + [o for distance in range(H - 1, 0, -1) for o in (distance, -distance)] + [0]
    place = {o % N: i for i, o in enumerate(offset)}
    column = [lax.rem(me + o % N, N) for o in offset]

    def at(way, distance):
        return place[(-distance if way == RIGHT else distance) % N]

    def block(i):
        return pl.ds(pl.multiple_of(column[i] * blk, blk), blk)

    loads = [
        pltpu.make_async_copy(wd.at[0], wdf.at[N - 1], lsem.at[0]),
        pltpu.make_async_copy(wu.at[0], wuf.at[N - 1], lsem.at[1]),
        pltpu.make_async_copy(incoming.at[0, 0], inc, lsem.at[2]),
        pltpu.make_async_copy(adopt, plan, lsem.at[3]),
        pltpu.make_async_copy(saved.at[0, 0, :, 0], x.at[0], lsem.at[4]),
        pltpu.make_async_copy(saved.at[0, 0, :, 1], x.at[1], lsem.at[5]),
    ]
    for load in loads:
        load.start()
    def head_copy(k, i):
        return pltpu.make_async_copy(head.at[k, 0, :, block(i)], g.at[k + 1, i], hsem.at[k, i])

    @pl.when(sec == S - 1)
    def _():
        for k in range(K - 1):
            for i in range(N):
                head_copy(k, i).start()

    barrier = pltpu.get_barrier_semaphore()
    for target in ((sec, left), (sec, right), (below, me), (above, me)):
        pl.semaphore_signal(barrier, inc=1, device_id=target, device_id_type=MESH)
    pl.semaphore_wait(barrier, 4)

    def remote(src, dst, send, recv, target):
        return pltpu.make_async_remote_copy(
            src_ref=src, dst_ref=dst, send_sem=send, recv_sem=recv, device_id=target, device_id_type=MESH
        )

    full = (wdf, wuf)

    def weight(w, way, hop):
        src, dst = full[w].at[at(way, hop - 1)], full[w].at[at(way, hop)]
        if hop == H:
            src, dst = src.at[pl.ds(way * half, half)], dst.at[pl.ds(way * half, half)]
        return remote(src, dst, ws.at[w, way, hop - 1], wr.at[w, way, hop - 1], side[way])

    def exchange(e, way, src, dst):
        return remote(src, dst.at[way], xs.at[e, way], xr.at[e, way], side[way])

    def add_h(i):
        inputs = x[:, :, :, block(i)].reshape(2 * rows, blk)
        hacc[...] += jnp.dot(inputs, wdf[i], preferred_element_type=F32)

    def add_c(i):
        cacc[...] += jnp.dot(g[0, i], wuf[i], preferred_element_type=F32)

    def pass_on(w, hop):
        for way in (RIGHT, LEFT):
            if hop > 1:
                weight(w, way, hop - 1).wait_recv()
            if hop <= H:
                weight(w, way, hop).start()

    def arrived(hop):
        return [(way, at(way, hop - 1)) for way in ((RIGHT, LEFT) if 1 < hop <= H else (RIGHT,))]

    def add_blocks(w, hop):
        for _, i in arrived(hop):
            (add_h, add_c)[w](i)

    def lower(hop, way, i):
        return remote(wdf.at[i], wda.at[i], ds.at[hop - 1, way], dr.at[hop - 1, way], (below, me))

    def lower_blocks(hop):
        @pl.when(sec > 0)
        def _():
            for way, i in arrived(hop):
                lower(hop, way, i).start()

    loads[0].wait()
    pass_on(DOWN, 1)
    loads[2].wait()
    inc_copies = [exchange(INC, way, inc.at[1], inc_in) for way in (RIGHT, LEFT)]
    for copy in inc_copies:
        copy.start()
    for load in (loads[1], loads[3], loads[4], loads[5]):
        load.wait()
    offsets = [plan[me, k, sec] for k in range(K)]
    first_g = remote(g.at[0], ga.at[0], gs, gr, (below, me))
    hacc[...] = jnp.zeros_like(hacc)
    cacc[...] = jnp.zeros_like(cacc)
    lower_blocks(1)
    add_blocks(DOWN, 1)
    for hop in range(2, H + 2):
        pass_on(DOWN, hop)
        lower_blocks(hop)
        add_blocks(DOWN, hop)
        if hop == 2:
            for copy in inc_copies:
                copy.wait_recv()
        if hop == H + 1:
            hb[...] = hacc[pl.ds(rows, rows)].astype(BF16)
            hid_copies = [exchange(HID, way, hb, h_in) for way in (RIGHT, LEFT)]
            for copy in hid_copies:
                copy.start()
        pass_on(UP, hop - 1)
        if hop == 2:
            d = offsets[0]
            for i in range(N):
                part = block(i)
                g[0, i] = jnp.where(
                    d == 0, inc[0, :, part], jnp.where(d == 1, inc_in[LEFT, :, part], inc_in[RIGHT, :, part])
                )

            @pl.when(sec > 0)
            def _():
                first_g.start()

        add_blocks(UP, hop - 1)

    for copy in hid_copies:
        copy.wait_recv()
    for k in range(K):
        d = offsets[k]
        part = pl.ds(k * T, T)
        h = jnp.where(d == 0, hacc[part], jnp.where(d == 1, h_in[LEFT, part], h_in[RIGHT, part]).astype(F32))
        gate = jax.nn.sigmoid(h)
        fac[k] = gate * (1.0 + h * (1.0 - gate))
        joins = jnp.where(d == 0, live[me], jnp.where(d == 1, live[right], live[left]))
        u[part] = jnp.where(joins == 1, h * gate, 0.0).astype(BF16)
    pass_on(UP, H + 1)
    add_blocks(UP, H + 1)

    ends = sorted({0, 3, (3 + N) // 2, N})
    pieces = list(zip(ends[:-1], ends[1:]))

    def back(inner, weights):
        return lax.dot_general(inner, weights, (((1,), (1,)), ((), ())), preferred_element_type=F32)

    def chain(k, n):
        part = pl.ds(pieces[n][0], pieces[n][1] - pieces[n][0])
        return remote(g.at[k, part], ga.at[k, part], cs.at[k - 1, n], cr.at[k - 1, n], (below, me))

    def chain_inner(k):
        return remote(inner_out.at[k], inner_in.at[k], ns.at[k], nr.at[k], (below, me))

    def send_inner(k):
        inner_out[k] = (fac[k] * cacc[...]).astype(BF16)

        @pl.when(sec > 0)
        def _():
            chain_inner(k).start()

    def next_g(k, n):
        @pl.when(sec < S - 1)
        def _():
            if n == 0:
                chain_inner(k).wait_recv()
            if k > 0:
                chain(k, n).wait_recv()
            inner = inner_in[k]
            for i in range(*pieces[n]):
                g[k + 1, i] = (ga[k, i].astype(F32) + back(inner, wda[i])).astype(BF16)

        if k + 1 < K - 1:
            @pl.when(sec > 0)
            def _():
                chain(k + 1, n).start()

    def next_c(k):
        total = jnp.zeros((T, R), F32)
        for i in range(N):
            total += jnp.dot(g[k + 1, i], wuf[i], preferred_element_type=F32)
        cacc[...] = total

    send_inner(0)

    @pl.when(sec == S - 1)
    def _():
        for k in range(K - 1):
            for i in range(N):
                head_copy(k, i).wait()

    @pl.when(sec < S - 1)
    def _():
        first_g.wait_recv()
        for hop in range(1, H + 2):
            for way, i in arrived(hop):
                lower(hop, way, i).wait_recv()

    for k in range(K - 2):
        for n in range(len(pieces)):
            next_g(k, n)
        next_c(k)
        send_inner(k + 1)

    def own(i, c):
        return lax.dot_general(
            g[:, i, :, c * half : (c + 1) * half].reshape(rows, half), u[...], (((0,), (0,)), ((), ())),
            preferred_element_type=F32,
        )

    quarter = half // 2

    def ring_sum(way, step, q):
        part = pl.ds(q * quarter, quarter)
        return remote(
            rs_out.at[way, step - 1, part], rs_in.at[way, step - 1, part],
            rss.at[way, step - 1, q], rsr.at[way, step - 1, q], side[way],
        )

    def sum_step(stream, step, fresh=False):
        first = isinstance(step, int) and step == 1
        terms = [own(0 if first else 2 * step - 3 + way, way ^ stream) for way in (RIGHT, LEFT)]
        for n in (0, 1):
            for way in (RIGHT, LEFT):
                q = 2 * (way ^ stream) + n
                part = pl.ds(q * quarter, quarter)
                value = terms[way][n * quarter : (n + 1) * quarter]
                if not fresh:
                    ring_sum(way, step - 1, q).wait_recv()
                    value = value + rs_in[way, step - 2, part].astype(F32)
                rs_out[way, step - 1, part] = value.astype(BF16)
                ring_sum(way, step, q).start()

    next_g(K - 2, 0)
    sum_step(0, 1, True)
    sum_step(1, 2, True)
    for n in range(1, len(pieces)):
        next_g(K - 2, n)
    next_c(K - 2)

    inner = (fac[K - 1] * cacc[...]).astype(BF16)
    for i in range(N):
        out[i] = (g[K - 1, i].astype(F32) + back(inner, wdf[i])).astype(BF16)
    leave_copies = [exchange(LEAVE, way, out, leave_in) for way in (RIGHT, LEFT)]
    for copy in leave_copies:
        copy.start()

    def sum_steps(step, _):
        sum_step(0, step)
        sum_step(1, step + 1)
        return 0

    lax.fori_loop(2, H, sum_steps, 0)
    sum_step(0, H)

    here = offsets[K - 1] == 0
    from_left, from_right = plan[left, K - 1, sec] == 1, plan[right, K - 1, sec] == -1
    nothing = jnp.zeros((T, blk), BF16)
    for i in range(N):
        leaving[0, 0, 0, :, block(i)] = jnp.where(here, out[i], nothing)
    for copy in leave_copies:
        copy.wait_recv()
    for i, o in enumerate(offset):
        leaving[0, 0, 1, :, block(i)] = jnp.where(
            from_left,
            leave_in[RIGHT, place[(o + 1) % N]],
            jnp.where(from_right, leave_in[LEFT, place[(o - 1) % N]], nothing),
        )

    scale = 1.0 / math.sqrt(N * K * T)
    for c in (0, 1):
        total = own(N - 1, c)
        for n in (0, 1):
            q = 2 * c + n
            part = pl.ds(q * quarter, quarter)
            value = total[n * quarter : (n + 1) * quarter]
            for way in (RIGHT, LEFT):
                ring_sum(way, H, q).wait_recv()
                value = value + rs_in[way, H - 1, part].astype(F32)
            grad[0, part] = (value * scale).astype(BF16)

    for w in (DOWN, UP):
        for way in (RIGHT, LEFT):
            for hop in range(1, H + 1):
                weight(w, way, hop).wait_send()
    for copy in inc_copies + hid_copies + leave_copies:
        copy.wait_send()

    @pl.when(sec > 0)
    def _():
        first_g.wait_send()
        for hop in range(1, H + 2):
            for way, i in arrived(hop):
                lower(hop, way, i).wait_send()
        for k in range(K - 1):
            chain_inner(k).wait_send()
        for k in range(1, K - 1):
            for n in range(len(pieces)):
                chain(k, n).wait_send()

    for way in (RIGHT, LEFT):
        for n in (0, 1):
            ring_sum(way, 1, 2 * way + n).wait_send()

    def drain_sums(step, _):
        for way in (RIGHT, LEFT):
            for q in range(4):
                ring_sum(way, step, q).wait_send()
        return 0

    lax.fori_loop(2, H + 1, drain_sums, 0)


def solution(mesh):
    S, N = mesh.shape["section"], mesh.shape["dp"]

    def body(saved, incoming, head, wd, wu, adopt, live):
        _, _, K, _, T, D = saved.shape
        blk, R = wd.shape[1:]
        H, rows = N // 2, K * T
        anywhere = pl.BlockSpec(memory_space=pltpu.HBM)
        vmem = pl.BlockSpec(memory_space=pltpu.VMEM)
        dma = pltpu.SemaphoreType.DMA
        return pl.pallas_call(
            functools.partial(kernel, S, N, K, T, D, R),
            out_shape=(
                jax.ShapeDtypeStruct((1, 1, 2, T, D), BF16),
                jax.ShapeDtypeStruct((1, blk, R), BF16),
            ),
            in_specs=[anywhere] * 6 + [pl.BlockSpec(memory_space=pltpu.SMEM)],
            out_specs=(vmem, vmem),
            scratch_shapes=[
                pltpu.VMEM((N, blk, R), BF16),
                pltpu.VMEM((N, blk, R), BF16),
                pltpu.VMEM((N, blk, R), BF16),
                pltpu.VMEM((2, K, T, D), BF16),
                pltpu.VMEM((2, T, D), BF16),
                pltpu.VMEM((2, T, D), BF16),
                pltpu.VMEM((2 * rows, R), F32),
                pltpu.VMEM((rows, R), BF16),
                pltpu.VMEM((2, rows, R), BF16),
                pltpu.VMEM((T, R), F32),
                pltpu.VMEM((K, N, T, blk), BF16),
                pltpu.VMEM((K - 1, N, T, blk), BF16),
                pltpu.VMEM((rows, R), BF16),
                pltpu.VMEM((K, T, R), F32),
                pltpu.VMEM((K - 1, T, R), BF16),
                pltpu.VMEM((K - 1, T, R), BF16),
                pltpu.VMEM((N, T, blk), BF16),
                pltpu.VMEM((2, N, T, blk), BF16),
                pltpu.VMEM((2, H, blk, R), BF16),
                pltpu.VMEM((2, H, blk, R), BF16),
                pltpu.SMEM((N, K, S), jnp.int32),
                dma((6,)),
                dma((K - 1, N)),
                dma((2, 2, H)),
                dma((2, 2, H)),
                dma((H + 1, 2)),
                dma((H + 1, 2)),
                dma((3, 2)),
                dma((3, 2)),
                dma,
                dma,
                dma((K - 1,)),
                dma((K - 1,)),
                dma((K - 2, 3)),
                dma((K - 2, 3)),
                dma((2, H, 4)),
                dma((2, H, 4)),
            ],
            compiler_params=pltpu.CompilerParams(
                collective_id=0, has_side_effects=True, vmem_limit_bytes=60 * 1024 * 1024
            ),
        )(saved, incoming, head, wd, wu, adopt.transpose(1, 2, 0), live)

    return jax.shard_map(
        body,
        mesh=mesh,
        in_specs=(
            P("section", "dp", None, None, None, None),
            P("section", "dp", None, None, None),
            P(None, "dp", None, None),
            P("section", "dp", None),
            P("section", "dp", None),
            P(),
            P(),
        ),
        out_specs=(P("section", "dp", None, None, None), P("section", "dp", None)),
        check_vma=False,
    )
```

time: 122 us -> 115 us (0.943)
  the two profiles are of different devices: /device:TPU:22 before, /device:TPU:1 now
where the time goes in v3:
time: 115 us
  Pallas kernels  111 us (97%)
  local copies, waits for them, and re-layouts  3.44 us (3%)
    pallas_call x1, Pallas kernels, body(): pl.pallas_call(functools.partial(kernel, S, N, K, T, D, R), out_shape=(ja...  111 us
    unnamed x2, local copies, waits for them, and re-layouts  3.44 us

profile of v3, /device:TPU:1, one launch (start us, length us, event | category | flops | bytes accessed | tf_op | source)
XLA Modules:
  0.0 115.0 jit_solution(10259189551629300170)
XLA Ops:
  0.6 110.9 %shard_map.86 = (bf16[1,1,2,32,4096]{4,3,2,1,0:T(8,128)(2,1)}, bf16[1,256,256]{2,1,0:T(8,128)(2,1)}) custom-call(bf16[1,1,4,2,32,4096]{5,4,3,2,1,0:T(8,128)(2,1)} %saved.1, bf16[1,1,2,32,4096]{4,3,2,1,0:T(8,128)(2,1)} %incoming.1, bf16[3,1,32,4096]{3,2,1,0:T(8,128)(2,1)} %head.1, bf16[1,256,256]{2,1,0:T(8,128)(2,1)} %wd.1, bf16[1,256,256]{2,1,0:T(8,128)(2,1)} %wu.1, ...), custom_call_target="tpu_custom_call" | custom-call | tf_op jit(solution)/shard_map/pallas_call | solution.py:345
  111.6 1.9 %copy.11 = bf16[1,1,2,32,4096]{4,3,2,1,0:T(8,128)(2,1)} copy(bf16[1,1,2,32,4096]{4,3,2,1,0:T(8,128)(2,1)} %get-tuple-element.4) | data formatting | bytes 1048576
  113.5 1.6 %copy.12 = bf16[1,256,256]{2,1,0:T(8,128)(2,1)} copy(bf16[1,256,256]{2,1,0:T(8,128)(2,1)} %get-tuple-element.5) | data formatting | bytes 262144

commit v4 on v3

--- a/solution.py
+++ b/solution.py
@@ -17,8 +17,8 @@
 
 def kernel(S, N, K, T, D, R,
            saved, incoming, head, wd, wu, adopt, live, leaving, grad,
-           wdf, wuf, wda, x, inc, inc_in, hacc, hb, h_in, cacc, g, ga, u, fac, inner_out, inner_in, out, leave_in,
-           rs_out, rs_in, plan, lsem, hsem, ws, wr, ds, dr, xs, xr, gs, gr, ns, nr, cs, cr, rss, rsr):
+           wdf, wuf, wda, x, inc, inc_in, hacc, hb, h_in, cacc, g, ga, u, fac, inner_out, inner_in, inner_side, spare, leave_in, pass_out, pass_in,
+           rs_out, rs_in, plan, lsem, hsem, ws, wr, ds, dr, xs, xr, gs, gr, ns, nr, cs, cr, spsem, is_, ir, ps, pr, rss, rsr):
     H, blk = N // 2, D // N
     half, rows = blk // 2, K * T
     sec, me = lax.axis_index("section"), lax.axis_index("dp")
@@ -54,6 +54,14 @@
         for k in range(K - 1):
             for i in range(N):
                 head_copy(k, i).start()
+
+    def spare_copy(i):
+        return pltpu.make_async_copy(head.at[sec, 0, :, block(i)], spare.at[i], spsem.at[i])
+
+    @pl.when(sec < K - 1)
+    def _():
+        for i in range(N):
+            spare_copy(i).start()
 
     barrier = pltpu.get_barrier_semaphore()
     for target in ((sec, left), (sec, right), (below, me), (above, me)):
@@ -173,12 +181,18 @@
     def chain_inner(k):
         return remote(inner_out.at[k], inner_in.at[k], ns.at[k], nr.at[k], (below, me))
 
+    def side_inner(k, way):
+        return remote(inner_out.at[k], inner_side.at[k, way], is_.at[k, way], ir.at[k, way], side[way])
+
     def send_inner(k):
         inner_out[k] = (fac[k] * cacc[...]).astype(BF16)
-
-        @pl.when(sec > 0)
-        def _():
-            chain_inner(k).start()
+        if k < K - 1:
+            @pl.when(sec > 0)
+            def _():
+                chain_inner(k).start()
+
+        for way in (RIGHT, LEFT):
+            side_inner(k, way).start()
 
     def next_g(k, n):
         @pl.when(sec < S - 1)
@@ -202,7 +216,52 @@
             total += jnp.dot(g[k + 1, i], wuf[i], preferred_element_type=F32)
         cacc[...] = total
 
+    def origin(way, src):
+        return exchange(LEAVE, way, src, leave_in)
+
     send_inner(0)
+
+    @pl.when(sec < K - 1)
+    def _():
+        for i in range(N):
+            spare_copy(i).wait()
+        for way in (RIGHT, LEFT):
+            origin(way, spare).start()
+
+    @pl.when(sec >= K - 1)
+    def _():
+        for way in (RIGHT, LEFT):
+            origin(way, g.at[0]).start()
+
+    def passing(k):
+        return remote(pass_out.at[k], pass_in.at[k], ps.at[k], pr.at[k], (below, me))
+
+    def leave_step(k):
+        behind = K - 1 - k
+        aim = lax.rem(sec + S - behind, S)
+        from_left, from_right = plan[left, K - 1, aim] == 1, plan[right, K - 1, aim] == -1
+        for way in (RIGHT, LEFT):
+            side_inner(k, way).wait_recv()
+        inner = jnp.where(from_left, inner_side[k, RIGHT], inner_side[k, LEFT])
+        inner = jnp.where(sec >= behind, inner, jnp.zeros_like(inner))
+        if k == 0:
+            for way in (RIGHT, LEFT):
+                origin(way, spare).wait_recv()
+        else:
+            passing(k - 1).wait_recv()
+        for i, o in enumerate(offset):
+            if k == 0:
+                before = jnp.where(from_left, leave_in[RIGHT, place[(o + 1) % N]], leave_in[LEFT, place[(o - 1) % N]])
+            else:
+                before = pass_in[k - 1, i]
+            value = (before.astype(F32) + back(inner, wdf[i])).astype(BF16)
+            if k < K - 1:
+                pass_out[k, i] = value
+            else:
+                nothing = jnp.zeros((T, blk), BF16)
+                leaving[0, 0, 1, :, block(i)] = jnp.where(from_left, value, jnp.where(from_right, value, nothing))
+        if k < K - 1:
+            passing(k).start()
 
     @pl.when(sec == S - 1)
     def _():
@@ -259,34 +318,23 @@
         next_g(K - 2, n)
     next_c(K - 2)
 
-    inner = (fac[K - 1] * cacc[...]).astype(BF16)
+    send_inner(K - 1)
+    here = offsets[K - 1] == 0
     for i in range(N):
-        out[i] = (g[K - 1, i].astype(F32) + back(inner, wdf[i])).astype(BF16)
-    leave_copies = [exchange(LEAVE, way, out, leave_in) for way in (RIGHT, LEFT)]
-    for copy in leave_copies:
-        copy.start()
+        value = (g[K - 1, i].astype(F32) + back(inner_out[K - 1], wdf[i])).astype(BF16)
+        leaving[0, 0, 0, :, block(i)] = jnp.where(here, value, jnp.zeros((T, blk), BF16))
+    leave_step(0)
 
     def sum_steps(step, _):
         sum_step(0, step)
         sum_step(1, step + 1)
         return 0
 
-    lax.fori_loop(2, H, sum_steps, 0)
+    steps = [min(2 + n * (H - 2) // (K - 1), H) for n in range(K)]
+    for k in range(1, K):
+        lax.fori_loop(steps[k - 1], steps[k], sum_steps, 0)
+        leave_step(k)
     sum_step(0, H)
-
-    here = offsets[K - 1] == 0
-    from_left, from_right = plan[left, K - 1, sec] == 1, plan[right, K - 1, sec] == -1
-    nothing = jnp.zeros((T, blk), BF16)
-    for i in range(N):
-        leaving[0, 0, 0, :, block(i)] = jnp.where(here, out[i], nothing)
-    for copy in leave_copies:
-        copy.wait_recv()
-    for i, o in enumerate(offset):
-        leaving[0, 0, 1, :, block(i)] = jnp.where(
-            from_left,
-            leave_in[RIGHT, place[(o + 1) % N]],
-            jnp.where(from_right, leave_in[LEFT, place[(o - 1) % N]], nothing),
-        )
 
     scale = 1.0 / math.sqrt(N * K * T)
     for c in (0, 1):
@@ -304,8 +352,14 @@
         for way in (RIGHT, LEFT):
             for hop in range(1, H + 1):
                 weight(w, way, hop).wait_send()
-    for copy in inc_copies + hid_copies + leave_copies:
+    for copy in inc_copies + hid_copies:
         copy.wait_send()
+    for way in (RIGHT, LEFT):
+        origin(way, spare).wait_send()
+        for k in range(K):
+            side_inner(k, way).wait_send()
+    for k in range(K - 1):
+        passing(k).wait_send()
 
     @pl.when(sec > 0)
     def _():
@@ -332,6 +386,11 @@
     lax.fori_loop(2, H + 1, drain_sums, 0)
 
 
+def hand_over(leaving, grad, leaving_out, grad_out):
+    leaving_out[...] = leaving[...]
+    grad_out[...] = grad[...]
+
+
 def solution(mesh):
     S, N = mesh.shape["section"], mesh.shape["dp"]
 
@@ -342,7 +401,7 @@
         anywhere = pl.BlockSpec(memory_space=pltpu.HBM)
         vmem = pl.BlockSpec(memory_space=pltpu.VMEM)
         dma = pltpu.SemaphoreType.DMA
-        return pl.pallas_call(
+        results = pl.pallas_call(
             functools.partial(kernel, S, N, K, T, D, R),
             out_shape=(
                 jax.ShapeDtypeStruct((1, 1, 2, T, D), BF16),
@@ -365,10 +424,13 @@
                 pltpu.VMEM((K - 1, N, T, blk), BF16),
                 pltpu.VMEM((rows, R), BF16),
                 pltpu.VMEM((K, T, R), F32),
+                pltpu.VMEM((K, T, R), BF16),
                 pltpu.VMEM((K - 1, T, R), BF16),
-                pltpu.VMEM((K - 1, T, R), BF16),
+                pltpu.VMEM((K, 2, T, R), BF16),
                 pltpu.VMEM((N, T, blk), BF16),
                 pltpu.VMEM((2, N, T, blk), BF16),
+                pltpu.VMEM((K - 1, N, T, blk), BF16),
+                pltpu.VMEM((K - 1, N, T, blk), BF16),
                 pltpu.VMEM((2, H, blk, R), BF16),
                 pltpu.VMEM((2, H, blk, R), BF16),
                 pltpu.SMEM((N, K, S), jnp.int32),
@@ -386,6 +448,11 @@
                 dma((K - 1,)),
                 dma((K - 2, 3)),
                 dma((K - 2, 3)),
+                dma((N,)),
+                dma((K, 2)),
+                dma((K, 2)),
+                dma((K - 1,)),
+                dma((K - 1,)),
                 dma((2, H, 4)),
                 dma((2, H, 4)),
             ],
@@ -393,6 +460,12 @@
                 collective_id=0, has_side_effects=True, vmem_limit_bytes=60 * 1024 * 1024
             ),
         )(saved, incoming, head, wd, wu, adopt.transpose(1, 2, 0), live)
+        return pl.pallas_call(
+            hand_over,
+            out_shape=tuple(jax.ShapeDtypeStruct(r.shape, r.dtype) for r in results),
+            in_specs=[vmem] * 2,
+            out_specs=(vmem, vmem),
+        )(*results)
 
     return jax.shard_map(
         body,

time: 115 us -> 110 us (0.957)
  local copies, waits for them, and re-layouts: 3.44 us -> 0 us
    unnamed x2 -> x0, local copies, waits for them, and re-layouts: 3.44 us -> none
    pallas_call x1, Pallas kernels: 111 us -> 108 us  [body(): pl.pallas_call(functools.partial(kernel, S, N, K, T, D, R), out_shape=(ja...]
    pallas_call x0 -> x1, Pallas kernels: none -> 1.93 us  [body(): pl.pallas_call(hand_over, out_shape=tuple((jax.ShapeDtypeStruct(r.shape,...]
where the time goes in v4:
time: 110 us
  Pallas kernels  110 us (100%)
    pallas_call x1, Pallas kernels, body(): pl.pallas_call(functools.partial(kernel, S, N, K, T, D, R), out_shape=(ja...  108 us

profile of v4, /device:TPU:1, one launch (start us, length us, event | category | flops | bytes accessed | tf_op | source)
XLA Modules:
  0.0 110.3 jit_solution(1145714085973171362)
XLA Ops:
  0.6 107.7 %shard_map.86 = (bf16[1,1,2,32,4096]{4,3,2,1,0:T(8,128)(2,1)}, bf16[1,256,256]{2,1,0:T(8,128)(2,1)}) custom-call(bf16[1,1,4,2,32,4096]{5,4,3,2,1,0:T(8,128)(2,1)} %saved.1, bf16[1,1,2,32,4096]{4,3,2,1,0:T(8,128)(2,1)} %incoming.1, bf16[3,1,32,4096]{3,2,1,0:T(8,128)(2,1)} %head.1, bf16[1,256,256]{2,1,0:T(8,128)(2,1)} %wd.1, bf16[1,256,256]{2,1,0:T(8,128)(2,1)} %wu.1, ...), custom_call_target="tpu_custom_call" | custom-call | tf_op jit(solution)/shard_map/pallas_call | solution.py:404
  108.4 1.9 %shard_map.87 = (bf16[1,1,2,32,4096]{4,3,2,1,0:T(8,128)(2,1)}, bf16[1,256,256]{2,1,0:T(8,128)(2,1)}) custom-call(bf16[1,1,2,32,4096]{4,3,2,1,0:T(8,128)(2,1)} %get-tuple-element.4.leaving, bf16[1,256,256]{2,1,0:T(8,128)(2,1)} %get-tuple-element.5.grad), custom_call_target="tpu_custom_call" | custom-call | tf_op jit(solution)/shard_map/pallas_call | solution.py:463

commit v5 on v4

--- a/solution.py
+++ b/solution.py
@@ -17,7 +17,7 @@
 
 def kernel(S, N, K, T, D, R,
            saved, incoming, head, wd, wu, adopt, live, leaving, grad,
-           wdf, wuf, wda, x, inc, inc_in, hacc, hb, h_in, cacc, g, ga, u, fac, inner_out, inner_in, inner_side, spare, leave_in, pass_out, pass_in,
+           wdf, wuf, wda, x, inc, inc_in, hacc, hb, h_in, cacc, above_c, mix, g, ga, u, fac, inner_out, inner_in, inner_side, spare, leave_in, pass_out, pass_in, part_back,
            rs_out, rs_in, plan, lsem, hsem, ws, wr, ds, dr, xs, xr, gs, gr, ns, nr, cs, cr, spsem, is_, ir, ps, pr, rss, rsr):
     H, blk = N // 2, D // N
     half, rows = blk // 2, K * T
@@ -108,6 +108,21 @@
     def lower(hop, way, i):
         return remote(wdf.at[i], wda.at[i], ds.at[hop - 1, way], dr.at[hop - 1, way], (below, me))
 
+    def add_mix(hop):
+        @pl.when(sec < S - 1)
+        def _():
+            for way, i in arrived(hop):
+                lower(hop, way, i).wait_recv()
+                mix[...] += lax.dot_general(
+                    wda[i], wuf[i], (((0,), (0,)), ((), ())), preferred_element_type=F32
+                )
+
+    def add_above(hop):
+        @pl.when(sec < S - 1)
+        def _():
+            for _, i in arrived(hop):
+                above_c[...] += jnp.dot(ga[0, i], wuf[i], preferred_element_type=F32)
+
     def lower_blocks(hop):
         @pl.when(sec > 0)
         def _():
@@ -126,6 +141,8 @@
     first_g = remote(g.at[0], ga.at[0], gs, gr, (below, me))
     hacc[...] = jnp.zeros_like(hacc)
     cacc[...] = jnp.zeros_like(cacc)
+    mix[...] = jnp.zeros_like(mix)
+    above_c[...] = jnp.zeros_like(above_c)
     lower_blocks(1)
     add_blocks(DOWN, 1)
     for hop in range(2, H + 2):
@@ -154,6 +171,17 @@
                 first_g.start()
 
         add_blocks(UP, hop - 1)
+        if hop > 3:
+            add_mix(hop - 3)
+        if hop == min(5, H + 1):
+            @pl.when(sec < S - 1)
+            def _():
+                first_g.wait_recv()
+
+            for earlier in range(1, hop - 1):
+                add_above(earlier)
+        if hop >= min(5, H + 1):
+            add_above(hop - 1)
 
     for copy in hid_copies:
         copy.wait_recv()
@@ -165,8 +193,12 @@
         fac[k] = gate * (1.0 + h * (1.0 - gate))
         joins = jnp.where(d == 0, live[me], jnp.where(d == 1, live[right], live[left]))
         u[part] = jnp.where(joins == 1, h * gate, 0.0).astype(BF16)
+    for hop in range(H - 1, H + 1):
+        add_mix(hop)
     pass_on(UP, H + 1)
     add_blocks(UP, H + 1)
+    add_above(H + 1)
+    add_mix(H + 1)
 
     ends = sorted({0, 3, (3 + N) // 2, N})
     pieces = list(zip(ends[:-1], ends[1:]))
@@ -197,13 +229,16 @@
     def next_g(k, n):
         @pl.when(sec < S - 1)
         def _():
-            if n == 0:
-                chain_inner(k).wait_recv()
             if k > 0:
                 chain(k, n).wait_recv()
             inner = inner_in[k]
             for i in range(*pieces[n]):
                 g[k + 1, i] = (ga[k, i].astype(F32) + back(inner, wda[i])).astype(BF16)
+            if 0 < k < K - 2:
+                total = above_c[...] if n > 0 else jnp.zeros((T, R), F32)
+                for i in range(*pieces[n]):
+                    total += jnp.dot(ga[k, i], wuf[i], preferred_element_type=F32)
+                above_c[...] = total
 
         if k + 1 < K - 1:
             @pl.when(sec > 0)
@@ -236,29 +271,44 @@
     def passing(k):
         return remote(pass_out.at[k], pass_in.at[k], ps.at[k], pr.at[k], (below, me))
 
-    def leave_step(k):
+    def adopted(k):
         behind = K - 1 - k
         aim = lax.rem(sec + S - behind, S)
         from_left, from_right = plan[left, K - 1, aim] == 1, plan[right, K - 1, aim] == -1
         for way in (RIGHT, LEFT):
             side_inner(k, way).wait_recv()
         inner = jnp.where(from_left, inner_side[k, RIGHT], inner_side[k, LEFT])
-        inner = jnp.where(sec >= behind, inner, jnp.zeros_like(inner))
-        if k == 0:
-            for way in (RIGHT, LEFT):
-                origin(way, spare).wait_recv()
-        else:
-            passing(k - 1).wait_recv()
+        return from_left, from_right, jnp.where(sec >= behind, inner, jnp.zeros_like(inner))
+
+    nothing = jnp.zeros((T, blk), BF16)
+
+    def leave_first():
+        picks = [adopted(k) for k in range(K - 1)]
+        inner = jnp.concatenate([inner_out[K - 1]] + [pick[2] for pick in picks], axis=0)
+        from_left = picks[0][0]
+        here = offsets[K - 1] == 0
+        for way in (RIGHT, LEFT):
+            origin(way, spare).wait_recv()
         for i, o in enumerate(offset):
-            if k == 0:
-                before = jnp.where(from_left, leave_in[RIGHT, place[(o + 1) % N]], leave_in[LEFT, place[(o - 1) % N]])
+            parts = back(inner, wdf[i])
+            own_out = (g[K - 1, i].astype(F32) + parts[:T]).astype(BF16)
+            leaving[0, 0, 0, :, block(i)] = jnp.where(here, own_out, nothing)
+            before = jnp.where(from_left, leave_in[RIGHT, place[(o + 1) % N]], leave_in[LEFT, place[(o - 1) % N]])
+            pass_out[0, i] = (before.astype(F32) + parts[T : 2 * T]).astype(BF16)
+            for k in range(1, K - 1):
+                part_back[k - 1, i] = parts[(k + 1) * T : (k + 2) * T]
+        passing(0).start()
+
+    def leave_step(k):
+        if k == K - 1:
+            from_left, from_right, inner = adopted(k)
+        passing(k - 1).wait_recv()
+        for i in range(N):
+            before = pass_in[k - 1, i].astype(F32)
+            if k < K - 1:
+                pass_out[k, i] = (before + part_back[k - 1, i]).astype(BF16)
             else:
-                before = pass_in[k - 1, i]
-            value = (before.astype(F32) + back(inner, wdf[i])).astype(BF16)
-            if k < K - 1:
-                pass_out[k, i] = value
-            else:
-                nothing = jnp.zeros((T, blk), BF16)
+                value = (before + back(inner, wdf[i])).astype(BF16)
                 leaving[0, 0, 1, :, block(i)] = jnp.where(from_left, value, jnp.where(from_right, value, nothing))
         if k < K - 1:
             passing(k).start()
@@ -269,18 +319,31 @@
             for i in range(N):
                 head_copy(k, i).wait()
 
-    @pl.when(sec < S - 1)
-    def _():
-        first_g.wait_recv()
-        for hop in range(1, H + 2):
-            for way, i in arrived(hop):
-                lower(hop, way, i).wait_recv()
+    def wait_inner(k):
+        @pl.when(sec < S - 1)
+        def _():
+            chain_inner(k).wait_recv()
+
+    def mixed_c(k):
+        @pl.when(sec < S - 1)
+        def _():
+            cacc[...] = above_c[...] + jnp.dot(inner_in[k], mix[...].astype(BF16), preferred_element_type=F32)
+
+        @pl.when(sec == S - 1)
+        def _():
+            next_c(k)
 
     for k in range(K - 2):
+        wait_inner(k)
+        if k == 0:
+            mixed_c(k)
+            send_inner(k + 1)
         for n in range(len(pieces)):
             next_g(k, n)
-        next_c(k)
-        send_inner(k + 1)
+        if k > 0:
+            mixed_c(k)
+            send_inner(k + 1)
+    wait_inner(K - 2)
 
     def own(i, c):
         return lax.dot_general(
@@ -319,11 +382,7 @@
     next_c(K - 2)
 
     send_inner(K - 1)
-    here = offsets[K - 1] == 0
-    for i in range(N):
-        value = (g[K - 1, i].astype(F32) + back(inner_out[K - 1], wdf[i])).astype(BF16)
-        leaving[0, 0, 0, :, block(i)] = jnp.where(here, value, jnp.zeros((T, blk), BF16))
-    leave_step(0)
+    leave_first()
 
     def sum_steps(step, _):
         sum_step(0, step)
@@ -420,6 +479,8 @@
                 pltpu.VMEM((rows, R), BF16),
                 pltpu.VMEM((2, rows, R), BF16),
                 pltpu.VMEM((T, R), F32),
+                pltpu.VMEM((T, R), F32),
+                pltpu.VMEM((R, R), F32),
                 pltpu.VMEM((K, N, T, blk), BF16),
                 pltpu.VMEM((K - 1, N, T, blk), BF16),
                 pltpu.VMEM((rows, R), BF16),
@@ -431,6 +492,7 @@
                 pltpu.VMEM((2, N, T, blk), BF16),
                 pltpu.VMEM((K - 1, N, T, blk), BF16),
                 pltpu.VMEM((K - 1, N, T, blk), BF16),
+                pltpu.VMEM((K - 2, N, T, blk), F32),
                 pltpu.VMEM((2, H, blk, R), BF16),
                 pltpu.VMEM((2, H, blk, R), BF16),
                 pltpu.SMEM((N, K, S), jnp.int32),

time: 110 us -> 109 us (level)
  Pallas kernels: 110 us -> 108 us
    pallas_call x1, Pallas kernels: 108 us -> 106 us  [body(): pl.pallas_call(functools.partial(kernel, S, N, K, T, D, R), out_shape=(ja...]
where the time goes in v5:
time: 109 us; the launch traced here: 108 us
  Pallas kernels  108 us (99%)
    pallas_call x1, Pallas kernels, body(): pl.pallas_call(functools.partial(kernel, S, N, K, T, D, R), out_shape=(ja...  106 us

profile of v5, /device:TPU:1, one launch (start us, length us, event | category | flops | bytes accessed | tf_op | source)
XLA Modules:
  0.0 108.2 jit_solution(3831957568986101596)
XLA Ops:
  0.6 105.7 %shard_map.86 = (bf16[1,1,2,32,4096]{4,3,2,1,0:T(8,128)(2,1)}, bf16[1,256,256]{2,1,0:T(8,128)(2,1)}) custom-call(bf16[1,1,4,2,32,4096]{5,4,3,2,1,0:T(8,128)(2,1)} %saved.1, bf16[1,1,2,32,4096]{4,3,2,1,0:T(8,128)(2,1)} %incoming.1, bf16[3,1,32,4096]{3,2,1,0:T(8,128)(2,1)} %head.1, bf16[1,256,256]{2,1,0:T(8,128)(2,1)} %wd.1, bf16[1,256,256]{2,1,0:T(8,128)(2,1)} %wu.1, ...), custom_call_target="tpu_custom_call" | custom-call | tf_op jit(solution)/shard_map/pallas_call | solution.py:463
  106.3 1.9 %shard_map.87 = (bf16[1,1,2,32,4096]{4,3,2,1,0:T(8,128)(2,1)}, bf16[1,256,256]{2,1,0:T(8,128)(2,1)}) custom-call(bf16[1,1,2,32,4096]{4,3,2,1,0:T(8,128)(2,1)} %get-tuple-element.4.leaving, bf16[1,256,256]{2,1,0:T(8,128)(2,1)} %get-tuple-element.5.grad), custom_call_target="tpu_custom_call" | custom-call | tf_op jit(solution)/shard_map/pallas_call | solution.py:525

commit v6 on v5

--- a/solution.py
+++ b/solution.py
@@ -395,6 +395,43 @@
         leave_step(k)
     sum_step(0, H)
 
+    for w in (DOWN, UP):
+        for way in (RIGHT, LEFT):
+            for hop in range(1, H + 1):
+                weight(w, way, hop).wait_send()
+    for copy in inc_copies + hid_copies:
+        copy.wait_send()
+    for way in (RIGHT, LEFT):
+        origin(way, spare).wait_send()
+        for k in range(K):
+            side_inner(k, way).wait_send()
+    for k in range(K - 1):
+        passing(k).wait_send()
+
+    @pl.when(sec > 0)
+    def _():
+        first_g.wait_send()
+        for hop in range(1, H + 2):
+            for way, i in arrived(hop):
+                lower(hop, way, i).wait_send()
+        for k in range(K - 1):
+            chain_inner(k).wait_send()
+        for k in range(1, K - 1):
+            for n in range(len(pieces)):
+                chain(k, n).wait_send()
+
+    for way in (RIGHT, LEFT):
+        for n in (0, 1):
+            ring_sum(way, 1, 2 * way + n).wait_send()
+
+    def drain_sums(step, _):
+        for way in (RIGHT, LEFT):
+            for q in range(4):
+                ring_sum(way, step, q).wait_send()
+        return 0
+
+    lax.fori_loop(2, H + 1, drain_sums, 0)
+
     scale = 1.0 / math.sqrt(N * K * T)
     for c in (0, 1):
         total = own(N - 1, c)
@@ -406,43 +443,6 @@
                 ring_sum(way, H, q).wait_recv()
                 value = value + rs_in[way, H - 1, part].astype(F32)
             grad[0, part] = (value * scale).astype(BF16)
-
-    for w in (DOWN, UP):
-        for way in (RIGHT, LEFT):
-            for hop in range(1, H + 1):
-                weight(w, way, hop).wait_send()
-    for copy in inc_copies + hid_copies:
-        copy.wait_send()
-    for way in (RIGHT, LEFT):
-        origin(way, spare).wait_send()
-        for k in range(K):
-            side_inner(k, way).wait_send()
-    for k in range(K - 1):
-        passing(k).wait_send()
-
-    @pl.when(sec > 0)
-    def _():
-        first_g.wait_send()
-        for hop in range(1, H + 2):
-            for way, i in arrived(hop):
-                lower(hop, way, i).wait_send()
-        for k in range(K - 1):
-            chain_inner(k).wait_send()
-        for k in range(1, K - 1):
-            for n in range(len(pieces)):
-                chain(k, n).wait_send()
-
-    for way in (RIGHT, LEFT):
-        for n in (0, 1):
-            ring_sum(way, 1, 2 * way + n).wait_send()
-
-    def drain_sums(step, _):
-        for way in (RIGHT, LEFT):
-            for q in range(4):
-                ring_sum(way, step, q).wait_send()
-        return 0
-
-    lax.fori_loop(2, H + 1, drain_sums, 0)
 
 
 def hand_over(leaving, grad, leaving_out, grad_out):

time: 109 us -> 109 us (level)
  no operation moved by 1% of the time
where the time goes in v6:
time: 109 us; the launch traced here: 108 us
  Pallas kernels  107 us (98%)
    pallas_call x1, Pallas kernels, body(): pl.pallas_call(functools.partial(kernel, S, N, K, T, D, R), out_shape=(ja...  105 us

profile of v6, /device:TPU:1, one launch (start us, length us, event | category | flops | bytes accessed | tf_op | source)
XLA Modules:
  0.0 108.0 jit_solution(10625019311614458169)
XLA Ops:
  0.6 105.4 %shard_map.86 = (bf16[1,1,2,32,4096]{4,3,2,1,0:T(8,128)(2,1)}, bf16[1,256,256]{2,1,0:T(8,128)(2,1)}) custom-call(bf16[1,1,4,2,32,4096]{5,4,3,2,1,0:T(8,128)(2,1)} %saved.1, bf16[1,1,2,32,4096]{4,3,2,1,0:T(8,128)(2,1)} %incoming.1, bf16[3,1,32,4096]{3,2,1,0:T(8,128)(2,1)} %head.1, bf16[1,256,256]{2,1,0:T(8,128)(2,1)} %wd.1, bf16[1,256,256]{2,1,0:T(8,128)(2,1)} %wu.1, ...), custom_call_target="tpu_custom_call" | custom-call | tf_op jit(solution)/shard_map/pallas_call | solution.py:463
  106.1 1.9 %shard_map.87 = (bf16[1,1,2,32,4096]{4,3,2,1,0:T(8,128)(2,1)}, bf16[1,256,256]{2,1,0:T(8,128)(2,1)}) custom-call(bf16[1,1,2,32,4096]{4,3,2,1,0:T(8,128)(2,1)} %get-tuple-element.4.leaving, bf16[1,256,256]{2,1,0:T(8,128)(2,1)} %get-tuple-element.5.grad), custom_call_target="tpu_custom_call" | custom-call | tf_op jit(solution)/shard_map/pallas_call | solution.py:525
